TPU v7x, 32 devices: a whole 2x2x4 slice. The times are simulated.
32 devices in a mesh: dp: 4 (over x, core), fsdp: 8 (over z, y).
Axes of the slice: x: 2, y: 2, z: 4, core: 2. Of those that a mesh axis runs over, the one named last changes fastest.
Arguments:
- inputs: bfloat16 [16, 1024, 768], P('dp', 'fsdp'), may hold values from -6 to 6
- segments: int32 [16, 1024], P('dp', 'fsdp'), may hold values from 0 to 3, as said below
- cotangent: bfloat16 [16, 1024, 768], P('dp', 'fsdp'), may hold values from -6 to 6
- qkv_weight: bfloat16 [768, 2304], P('fsdp'), may hold values from -0.21875 to 0.21875
- query_bias: bfloat16 [768], P('fsdp'), may hold values from -3 to 3
- value_bias: bfloat16 [768], P('fsdp'), may hold values from -3 to 3
- out_weight: bfloat16 [768, 768], P('fsdp'), may hold values from -0.875 to 0.875
- out_bias: bfloat16 [768], P('fsdp'), may hold values from -1.75 to 1.75
- norm1_gain: bfloat16 [768], P('fsdp'), may hold values from 0.099609375 to 1.8984375
- norm1_shift: bfloat16 [768], P('fsdp'), may hold values from -3 to 3
- up_weight: bfloat16 [768, 3072], P('fsdp'), may hold values from -0.21875 to 0.21875
- up_bias: bfloat16 [3072], P('fsdp'), may hold values from -3 to 3
- down_weight: bfloat16 [3072, 768], P('fsdp'), may hold values from -0.109375 to 0.109375
- down_bias: bfloat16 [768], P('fsdp'), may hold values from -1.75 to 1.75
- norm2_gain: bfloat16 [768], P('fsdp'), may hold values from 0.099609375 to 1.8984375
- norm2_shift: bfloat16 [768], P('fsdp'), may hold values from -3 to 3
Outputs:
- output: bfloat16 [16, 1024, 768], P('dp', 'fsdp')
- d_inputs: bfloat16 [16, 1024, 768], P('dp', 'fsdp')
- d_qkv_weight: float32 [768, 2304], P('fsdp')
- d_query_bias: float32 [768], P('fsdp')
- d_value_bias: float32 [768], P('fsdp')
- d_out_weight: float32 [768, 768], P('fsdp')
- d_out_bias: float32 [768], P('fsdp')
- d_norm1_gain: float32 [768], P('fsdp')
- d_norm1_shift: float32 [768], P('fsdp')
- d_up_weight: float32 [768, 3072], P('fsdp')
- d_up_bias: float32 [3072], P('fsdp')
- d_down_weight: float32 [3072, 768], P('fsdp')
- d_down_bias: float32 [768], P('fsdp')
- d_norm2_gain: float32 [768], P('fsdp')
- d_norm2_shift: float32 [768], P('fsdp')
Inputs may be any that keep to these rules, and one draw needn't show every extreme that they name: `segments`: within each sequence the numbers start at 0 and never fall; in each group of 4 consecutive sequences one sequence is a single document.
All inputs are finite; a program needn't handle non-finite values.
Results may differ from a plain program's by a relative error of at most 0.02.
Values may be sent and summed in bfloat16 or wider, within the bound.
No kernel may reach another device: no remote copies, remote signals or barrier semaphores. Data moves between devices by JAX's collectives and lax.ppermute only.
A program may use at most 384 MiB of HBM per device.

v0:
```python
import jax
import jax.numpy as jnp
from jax import lax
from jax.sharding import PartitionSpec as P

HEAD_DIM = 64


def layer_normalize(values, norm_gain, norm_shift):
    centered_input = values - jnp.mean(values, axis=-1, keepdims=True)
    spread = jnp.mean(centered_input * centered_input, axis=-1, keepdims=True)
    inverse_deviation = lax.rsqrt(spread + 1e-05)
    standardized = centered_input * inverse_deviation
    return (standardized, inverse_deviation, standardized * norm_gain + norm_shift)


def norm_backward(output_gradient, standardized, inverse_deviation, norm_gain):
    normalized_gradient = output_gradient * norm_gain
    input_gradient = inverse_deviation * (
        normalized_gradient
        - jnp.mean(normalized_gradient, axis=-1, keepdims=True)
        - standardized * jnp.mean(normalized_gradient * standardized, axis=-1, keepdims=True)
    )
    return (
        input_gradient,
        jnp.sum(output_gradient * standardized, axis=0),
        jnp.sum(output_gradient, axis=0),
    )


def split_pairs(tensor):
    count = tensor.shape[0]
    return tensor.reshape(count, -1, 2, HEAD_DIM).transpose(1, 0, 2, 3)


def join_pairs(tensor):
    count = tensor.shape[1]
    return tensor.transpose(1, 0, 2, 3).reshape(count, -1)


def attend_sequence(item):
    queries, keys, values, allowed = item
    scale = HEAD_DIM ** (-0.5)

    def attend_pair(pair):
        q_pair, k_pair, v_pair = pair
        scores = (
            jnp.einsum("qhd,khd->hqk", q_pair, k_pair, preferred_element_type=jnp.float32) * scale
        )
        scores = jnp.where(allowed[None], scores, jnp.float32(-1e30))
        top = jnp.max(scores, axis=-1, keepdims=True)
        expo = jnp.exp(scores - top)
        total = jnp.sum(expo, axis=-1, keepdims=True)
        probs = (expo / total).astype(jnp.bfloat16)
        mixed = jnp.einsum("hqk,khd->qhd", probs, v_pair, preferred_element_type=jnp.float32)
        return (mixed, (top + jnp.log(total))[..., 0])

    mixed, logsum = lax.map(
        attend_pair, (split_pairs(queries), split_pairs(keys), split_pairs(values))
    )
    return (join_pairs(mixed), logsum)


def attend_back(item):
    queries, keys, values, allowed, d_mixed, logsum = item
    scale = HEAD_DIM ** (-0.5)

    def back_pair(pair):
        q_pair, k_pair, v_pair, d_pair, l_pair = pair
        scores = (
            jnp.einsum("qhd,khd->hqk", q_pair, k_pair, preferred_element_type=jnp.float32) * scale
        )
        scores = jnp.where(allowed[None], scores, jnp.float32(-1e30))
        probs = jnp.exp(scores - l_pair[..., None])
        d_probs = jnp.einsum("qhd,khd->hqk", d_pair, v_pair, preferred_element_type=jnp.float32)
        delta = jnp.sum(probs * d_probs, axis=-1, keepdims=True)
        d_scores = (probs * (d_probs - delta)).astype(jnp.bfloat16)
        d_query = (
            jnp.einsum("hqk,khd->qhd", d_scores, k_pair, preferred_element_type=jnp.float32) * scale
        )
        d_key = (
            jnp.einsum("hqk,qhd->khd", d_scores, q_pair, preferred_element_type=jnp.float32) * scale
        )
        d_value = jnp.einsum(
            "hqk,qhd->khd", probs.astype(jnp.bfloat16), d_pair, preferred_element_type=jnp.float32
        )
        return (d_query, d_key, d_value, delta[..., 0])

    d_query, d_key, d_value, delta = lax.map(
        back_pair,
        (
            split_pairs(queries),
            split_pairs(keys),
            split_pairs(values),
            split_pairs(d_mixed),
            logsum,
        ),
    )
    return (join_pairs(d_query), join_pairs(d_key), join_pairs(d_value), delta)


def local(
    inputs,
    segments,
    cotangent,
    qkv_weight,
    query_bias,
    value_bias,
    out_weight,
    out_bias,
    norm1_gain,
    norm1_shift,
    up_weight,
    up_bias,
    down_weight,
    down_bias,
    norm2_gain,
    norm2_shift,
):
    seqs, block, width = inputs.shape
    rows = seqs * block
    single_float32 = jnp.float32
    bf16 = jnp.bfloat16
    attn_local = (qkv_weight, out_weight, query_bias, value_bias, out_bias, norm1_gain, norm1_shift)
    mlp_local = (up_weight, down_weight, up_bias, down_bias, norm2_gain, norm2_shift)
    attn_full = (
        lax.all_gather(attn_local[0], "fsdp", axis=0, tiled=True),
        lax.all_gather(attn_local[1], "fsdp", axis=0, tiled=True),
        lax.all_gather(attn_local[2], "fsdp", axis=0, tiled=True),
        lax.all_gather(attn_local[3], "fsdp", axis=0, tiled=True),
        lax.all_gather(attn_local[4], "fsdp", axis=0, tiled=True),
        lax.all_gather(attn_local[5], "fsdp", axis=0, tiled=True),
        lax.all_gather(attn_local[6], "fsdp", axis=0, tiled=True),
    )
    w_qkv, w_out, b_query, b_value, b_out, first_gain, first_shift = attn_full
    residual_stream = inputs.astype(single_float32).reshape(rows, width)
    standardized1, inverse_deviation1, first_normed = layer_normalize(
        residual_stream, first_gain.astype(single_float32), first_shift.astype(single_float32)
    )
    hidden1 = first_normed.astype(bf16)
    joined = jnp.dot(hidden1, w_qkv, preferred_element_type=single_float32)
    queries = (joined[:, :width] + b_query.astype(single_float32)).astype(bf16)
    keys = joined[:, width : 2 * width].astype(bf16)
    values = (joined[:, 2 * width :] + b_value.astype(single_float32)).astype(bf16)
    key_seq = keys.reshape(seqs, block, width)
    value_seq = values.reshape(seqs, block, width)
    all_keys, all_values = (
        lax.all_gather(key_seq, "fsdp", axis=1, tiled=True),
        lax.all_gather(value_seq, "fsdp", axis=1, tiled=True),
    )
    all_segs = lax.all_gather(segments, "fsdp", axis=1, tiled=True)
    length = all_keys.shape[1]
    own_pos = lax.axis_index("fsdp") * block + jnp.arange(block, dtype=jnp.int32)
    every_pos = jnp.arange(length, dtype=jnp.int32)
    allowed = (every_pos[None, None, :] <= own_pos[None, :, None]) & (
        all_segs[:, None, :] == segments[:, :, None]
    )
    query_seq = queries.reshape(seqs, block, width)
    mixed, logsum = lax.map(attend_sequence, (query_seq, all_keys, all_values, allowed))
    mixed_low = mixed.reshape(rows, width).astype(bf16)
    midway_state = (
        residual_stream
        + jnp.dot(mixed_low, w_out, preferred_element_type=single_float32)
        + b_out.astype(single_float32)
    )
    mlp_full = (
        lax.all_gather(mlp_local[0], "fsdp", axis=0, tiled=True),
        lax.all_gather(mlp_local[1], "fsdp", axis=0, tiled=True),
        lax.all_gather(mlp_local[2], "fsdp", axis=0, tiled=True),
        lax.all_gather(mlp_local[3], "fsdp", axis=0, tiled=True),
        lax.all_gather(mlp_local[4], "fsdp", axis=0, tiled=True),
        lax.all_gather(mlp_local[5], "fsdp", axis=0, tiled=True),
    )
    w_up, w_down, b_up, b_down, second_gain, second_shift = mlp_full
    standardized2, inverse_deviation2, second_normed = layer_normalize(
        midway_state, second_gain.astype(single_float32), second_shift.astype(single_float32)
    )
    hidden2 = second_normed.astype(bf16)
    pre_act = jnp.dot(hidden2, w_up, preferred_element_type=single_float32) + b_up.astype(
        single_float32
    )
    activ = jax.nn.gelu(pre_act, approximate=True).astype(bf16)
    result = (
        midway_state
        + jnp.dot(activ, w_down, preferred_element_type=single_float32)
        + b_down.astype(single_float32)
    )
    output = result.astype(bf16).reshape(seqs, block, width)
    grad_low = cotangent.reshape(rows, width)
    grad_out = grad_low.astype(single_float32)
    w_up, w_down, b_up, b_down, second_gain, second_shift = (
        lax.all_gather(mlp_local[0], "fsdp", axis=0, tiled=True),
        lax.all_gather(mlp_local[1], "fsdp", axis=0, tiled=True),
        lax.all_gather(mlp_local[2], "fsdp", axis=0, tiled=True),
        lax.all_gather(mlp_local[3], "fsdp", axis=0, tiled=True),
        lax.all_gather(mlp_local[4], "fsdp", axis=0, tiled=True),
        lax.all_gather(mlp_local[5], "fsdp", axis=0, tiled=True),
    )
    d_down_w = jnp.dot(activ.T, grad_low, preferred_element_type=single_float32)
    d_down_b = jnp.sum(grad_out, axis=0)
    d_activ = jnp.dot(grad_low, w_down.T, preferred_element_type=single_float32)
    gelu_back = jax.vjp(lambda values_in: jax.nn.gelu(values_in, approximate=True), pre_act)[1]
    d_pre = gelu_back(d_activ)[0].astype(bf16)
    d_up_w = jnp.dot(hidden2.T, d_pre, preferred_element_type=single_float32)
    d_up_b = jnp.sum(d_pre.astype(single_float32), axis=0)
    hidden2_gradient = jnp.dot(d_pre, w_up.T, preferred_element_type=single_float32)
    norm2_gradient, second_gain_gradient, second_shift_gradient = norm_backward(
        hidden2_gradient, standardized2, inverse_deviation2, second_gain.astype(single_float32)
    )
    d_middle = grad_out + norm2_gradient
    w_qkv, w_out, b_query, b_value, b_out, first_gain, first_shift = (
        lax.all_gather(attn_local[0], "fsdp", axis=0, tiled=True),
        lax.all_gather(attn_local[1], "fsdp", axis=0, tiled=True),
        lax.all_gather(attn_local[2], "fsdp", axis=0, tiled=True),
        lax.all_gather(attn_local[3], "fsdp", axis=0, tiled=True),
        lax.all_gather(attn_local[4], "fsdp", axis=0, tiled=True),
        lax.all_gather(attn_local[5], "fsdp", axis=0, tiled=True),
        lax.all_gather(attn_local[6], "fsdp", axis=0, tiled=True),
    )
    d_branch = d_middle.astype(bf16)
    d_out_w = jnp.dot(mixed_low.T, d_branch, preferred_element_type=single_float32)
    d_out_b = jnp.sum(d_branch.astype(single_float32), axis=0)
    d_mixed = jnp.dot(d_branch, w_out.T, preferred_element_type=single_float32).astype(bf16)
    d_mixed_seq = d_mixed.reshape(seqs, block, width)
    d_query, d_key_all, d_value_all, delta = lax.map(
        attend_back, (query_seq, all_keys, all_values, allowed, d_mixed_seq, logsum)
    )
    d_key, d_value = (
        lax.psum_scatter(
            d_key_all.astype(jnp.bfloat16), "fsdp", scatter_dimension=1, tiled=True
        ).astype(jnp.float32),
        lax.psum_scatter(
            d_value_all.astype(jnp.bfloat16), "fsdp", scatter_dimension=1, tiled=True
        ).astype(jnp.float32),
    )
    d_query = d_query.reshape(rows, width).astype(bf16)
    d_key = d_key.reshape(rows, width).astype(bf16)
    d_value = d_value.reshape(rows, width).astype(bf16)
    d_joined = jnp.concatenate([d_query, d_key, d_value], axis=1)
    d_qkv_w = jnp.dot(hidden1.T, d_joined, preferred_element_type=single_float32)
    d_query_b = jnp.sum(d_query.astype(single_float32), axis=0)
    d_value_b = jnp.sum(d_value.astype(single_float32), axis=0)
    hidden1_gradient = jnp.dot(d_joined, w_qkv.T, preferred_element_type=single_float32)
    norm1_gradient, first_gain_gradient, first_shift_gradient = norm_backward(
        hidden1_gradient, standardized1, inverse_deviation1, first_gain.astype(single_float32)
    )
    d_inputs = (d_middle + norm1_gradient).astype(bf16).reshape(seqs, block, width)
    partial_grads = (
        d_qkv_w,
        d_query_b,
        d_value_b,
        d_out_w,
        d_out_b,
        first_gain_gradient,
        first_shift_gradient,
        d_up_w,
        d_up_b,
        d_down_w,
        d_down_b,
        second_gain_gradient,
        second_shift_gradient,
    )
    shards = (
        lax.psum_scatter(
            partial_grads[0].astype(jnp.bfloat16), "fsdp", scatter_dimension=0, tiled=True
        ).astype(jnp.float32),
        lax.psum_scatter(
            partial_grads[1].astype(jnp.bfloat16), "fsdp", scatter_dimension=0, tiled=True
        ).astype(jnp.float32),
        lax.psum_scatter(
            partial_grads[2].astype(jnp.bfloat16), "fsdp", scatter_dimension=0, tiled=True
        ).astype(jnp.float32),
        lax.psum_scatter(
            partial_grads[3].astype(jnp.bfloat16), "fsdp", scatter_dimension=0, tiled=True
        ).astype(jnp.float32),
        lax.psum_scatter(
            partial_grads[4].astype(jnp.bfloat16), "fsdp", scatter_dimension=0, tiled=True
        ).astype(jnp.float32),
        lax.psum_scatter(
            partial_grads[5].astype(jnp.bfloat16), "fsdp", scatter_dimension=0, tiled=True
        ).astype(jnp.float32),
        lax.psum_scatter(
            partial_grads[6].astype(jnp.bfloat16), "fsdp", scatter_dimension=0, tiled=True
        ).astype(jnp.float32),
        lax.psum_scatter(
            partial_grads[7].astype(jnp.bfloat16), "fsdp", scatter_dimension=0, tiled=True
        ).astype(jnp.float32),
        lax.psum_scatter(
            partial_grads[8].astype(jnp.bfloat16), "fsdp", scatter_dimension=0, tiled=True
        ).astype(jnp.float32),
        lax.psum_scatter(
            partial_grads[9].astype(jnp.bfloat16), "fsdp", scatter_dimension=0, tiled=True
        ).astype(jnp.float32),
        lax.psum_scatter(
            partial_grads[10].astype(jnp.bfloat16), "fsdp", scatter_dimension=0, tiled=True
        ).astype(jnp.float32),
        lax.psum_scatter(
            partial_grads[11].astype(jnp.bfloat16), "fsdp", scatter_dimension=0, tiled=True
        ).astype(jnp.float32),
        lax.psum_scatter(
            partial_grads[12].astype(jnp.bfloat16), "fsdp", scatter_dimension=0, tiled=True
        ).astype(jnp.float32),
    )
    totals = (
        lax.psum(shards[0].astype(jnp.bfloat16), "dp").astype(jnp.float32),
        lax.psum(shards[1].astype(jnp.bfloat16), "dp").astype(jnp.float32),
        lax.psum(shards[2].astype(jnp.bfloat16), "dp").astype(jnp.float32),
        lax.psum(shards[3].astype(jnp.bfloat16), "dp").astype(jnp.float32),
        lax.psum(shards[4].astype(jnp.bfloat16), "dp").astype(jnp.float32),
        lax.psum(shards[5].astype(jnp.bfloat16), "dp").astype(jnp.float32),
        lax.psum(shards[6].astype(jnp.bfloat16), "dp").astype(jnp.float32),
        lax.psum(shards[7].astype(jnp.bfloat16), "dp").astype(jnp.float32),
        lax.psum(shards[8].astype(jnp.bfloat16), "dp").astype(jnp.float32),
        lax.psum(shards[9].astype(jnp.bfloat16), "dp").astype(jnp.float32),
        lax.psum(shards[10].astype(jnp.bfloat16), "dp").astype(jnp.float32),
        lax.psum(shards[11].astype(jnp.bfloat16), "dp").astype(jnp.float32),
        lax.psum(shards[12].astype(jnp.bfloat16), "dp").astype(jnp.float32),
    )
    return (output, d_inputs) + tuple(totals)


def solution(mesh):
    in_specs = (
        P("dp", "fsdp", None),
        P("dp", "fsdp"),
        P("dp", "fsdp", None),
        P("fsdp", None),
        P("fsdp"),
        P("fsdp"),
        P("fsdp", None),
        P("fsdp"),
        P("fsdp"),
        P("fsdp"),
        P("fsdp", None),
        P("fsdp"),
        P("fsdp", None),
        P("fsdp"),
        P("fsdp"),
        P("fsdp"),
    )
    out_specs = (
        P("dp", "fsdp", None),
        P("dp", "fsdp", None),
        P("fsdp", None),
        P("fsdp"),
        P("fsdp"),
        P("fsdp", None),
        P("fsdp"),
        P("fsdp"),
        P("fsdp"),
        P("fsdp", None),
        P("fsdp"),
        P("fsdp", None),
        P("fsdp"),
        P("fsdp"),
        P("fsdp"),
    )
    return jax.shard_map(local, mesh=mesh, in_specs=in_specs, out_specs=out_specs, check_vma=False)
```

profile of v0, /device:TPU:9, one launch (start us, length us, event | category | flops | bytes accessed | tf_op | source)
XLA Modules:
  0.0 1330.3 jit_solution(651427056947203397)
XLA Ops:
  15.8 27.7 %all-reduce.18 = (bf16[768]{0:T(1024)(128)(2,1)S(1)}, bf16[768]{0:T(1024)(128)(2,1)S(1)}, bf16[768]{0:T(1024)(128)(2,1)S(1)}, bf16[768]{0:T(1024)(128)(2,1)S(1)}...) all-reduce(bf16[768]{0:T(1024)(128)(2,1)S(1)} %dynamic-update-slice, ...), channel_id=1, replica_groups=mesh['dp'=4,'fsdp'=8] {'fsdp'}, use_global_device_ids=true, to_apply=%add.1 | all-reduce | flops 5376 | bytes 21504
  46.3 29.1 %all-gather.8.cloned.1.call-done = bf16[768,2304]{1,0:T(8,128)(2,1)} async-done(((bf16[96,2304]{1,0:T(8,128)(2,1)}), bf16[768,2304]{1,0:T(8,128)(2,1)}) %all-gather.8.cloned.1.call-update) | async-done | bytes 3538960 | tf_op jit(solution)/shard_map/all_gather | solution.py:127
  88.1 21.7 %all-gather = bf16[8,1,384]{2,1,0:T(2,128)(2,1)S(1)} all-gather(bf16[1,1,384]{2,1,0:T(2,128)(2,1)S(1)} %reshape.256), channel_id=1, replica_groups=mesh['dp'=4,'fsdp'=8] {'fsdp'}, dimensions={0}, use_global_device_ids=true | all-gather | bytes 6912 | tf_op jit(solution)/shard_map/all_gather | solution.py:169
  109.9 22.4 %all_gather.61 = s32[4,1024]{1,0:T(4,128)S(1)} all-gather(s32[4,128]{1,0:T(4,128)S(1)} %copy-done.22), channel_id=1, replica_groups=mesh['dp'=4,'fsdp'=8] {'fsdp'}, dimensions={1}, use_global_device_ids=true | all-gather | bytes 18432 | tf_op jit(solution)/shard_map/all_gather | solution.py:151
  134.8 46.4 %all-gather.10.cloned.1.call-done = bf16[4,1024,768]{1,2,0:T(8,128)(2,1)} async-done(((bf16[4,128,768]{1,2,0:T(8,128)(2,1)}), bf16[4,1024,768]{1,2,0:T(8,128)(2,1)}) %all-gather.10.cloned.1.call-update) | async-done | bytes 6291472 | tf_op jit(solution)/shard_map/all_gather | solution.py:148
  181.2 100.7 %all-gather.12.cloned.1.call-done = bf16[4,1024,768]{1,2,0:T(8,128)(2,1)} async-done(((bf16[4,128,768]{1,2,0:T(8,128)(2,1)}), bf16[4,1024,768]{1,2,0:T(8,128)(2,1)}) %all-gather.12.cloned.1.call-update) | async-done | bytes 6291472 | tf_op jit(solution)/shard_map/all_gather | solution.py:149
  282.8 67.7 %while.53 = (s32[]{:T(128)}, bf16[4,128,768]{2,1,0:T(8,128)(2,1)}, f32[4,6,2,128]{3,2,1,0:T(2,128)S(1)}, bf16[4,128,768]{1,2,0:T(8,128)(2,1)}, bf16[4,1024,768]{...) while((s32[]{:T(128)}, bf16[4,128,768]{2,1,0:T(8,128)(2,1)}, ...), condition=%wide.region_7.8_spmd, body=%wide.region_2.7_spmd.sunk | while | flops 69205760 | bytes 11655466 | solution.py:159
  286.9 11.0 while.56
  303.7 11.0 while.56
  320.7 11.0 while.56
  337.8 11.0 while.56
  353.5 50.8 %all-gather.16.cloned.1.call-done = bf16[768,3072]{1,0:T(8,128)(2,1)} async-done(((bf16[96,3072]{1,0:T(8,128)(2,1)}), bf16[768,3072]{1,0:T(8,128)(2,1)}) %all-gather.16.cloned.1.call-update) | async-done | bytes 4718608 | tf_op jit(solution)/shard_map/all_gather | solution.py:167
  404.3 7.0 fusion.72
  411.4 73.0 %all-gather.18.cloned.1.call-done = bf16[3072,768]{1,0:T(8,128)(2,1)} async-done(((bf16[384,768]{1,0:T(8,128)(2,1)}), bf16[3072,768]{1,0:T(8,128)(2,1)}) %all-gather.18.cloned.1.call-update) | async-done | bytes 4718608 | tf_op jit(solution)/shard_map/all_gather | solution.py:168
  484.4 9.2 fusion.73
  500.6 183.3 %while.55 = (s32[]{:T(128)}, bf16[4,128,768]{2,1,0:T(8,128)(2,1)}, bf16[4,1024,768]{2,1,0:T(8,128)(2,1)}, bf16[4,1024,768]{2,1,0:T(8,128)(2,1)}, bf16[4,128,768]...) while((s32[]{:T(128)}, bf16[4,128,768]{2,1,0:T(8,128)(2,1)}, ...), condition=%wide.region_16.17_spmd, body=%wide.region_12.16_spmd.sunk | while | flops 170278656 | bytes 31938968 | solution.py:225
  507.3 32.8 %while.57 = (s32[]{:T(128)}, bf16[6,128,2,64]{1,3,2,0:T(8,128)(2,1)}, bf16[6,1024,2,64]{1,3,2,0:T(8,128)(2,1)}, bf16[6,1024,2,64]{1,3,2,0:T(8,128)(2,1)}, bf16[6...) while((s32[]{:T(128)}, ...), condition=%wide.region_15.15_spmd, body=%wide.region_13.14_spmd.sunk | while | flops 170278656 | bytes 10037369 | solution.py:89
  553.2 32.8 %while.57 = (s32[]{:T(128)}, bf16[6,128,2,64]{1,3,2,0:T(8,128)(2,1)}, bf16[6,1024,2,64]{1,3,2,0:T(8,128)(2,1)}, bf16[6,1024,2,64]{1,3,2,0:T(8,128)(2,1)}, bf16[6...) while((s32[]{:T(128)}, ...), condition=%wide.region_15.15_spmd, body=%wide.region_13.14_spmd.sunk | while | flops 170278656 | bytes 10037369 | solution.py:89
  599.0 32.8 %while.57 = (s32[]{:T(128)}, bf16[6,128,2,64]{1,3,2,0:T(8,128)(2,1)}, bf16[6,1024,2,64]{1,3,2,0:T(8,128)(2,1)}, bf16[6,1024,2,64]{1,3,2,0:T(8,128)(2,1)}, bf16[6...) while((s32[]{:T(128)}, ...), condition=%wide.region_15.15_spmd, body=%wide.region_13.14_spmd.sunk | while | flops 170278656 | bytes 10037369 | solution.py:89
  644.9 32.8 %while.57 = (s32[]{:T(128)}, bf16[6,128,2,64]{1,3,2,0:T(8,128)(2,1)}, bf16[6,1024,2,64]{1,3,2,0:T(8,128)(2,1)}, bf16[6,1024,2,64]{1,3,2,0:T(8,128)(2,1)}, bf16[6...) while((s32[]{:T(128)}, ...), condition=%wide.region_15.15_spmd, body=%wide.region_13.14_spmd.sunk | while | flops 170278656 | bytes 10037369 | solution.py:89
  688.4 6.5 convolution_convert_fusion.1
  696.1 8.7 convolution_convert_fusion
  704.9 96.4 %reduce-scatter.9.cloned.1.call-done = bf16[4,128,768]{2,1,0:T(8,128)(2,1)} async-done(((bf16[4,1024,768]{2,1,0:T(8,128)(2,1)}), bf16[4,128,768]{2,1,0:T(8,128)(2,1)}) %reduce-scatter.9.cloned.1.call-update) | async-done | bytes 786448 | tf_op jit(solution)/shard_map/reduce_scatter | solution.py:232
  801.3 120.8 %reduce-scatter.7.cloned.1.call-done = bf16[4,128,768]{2,1,0:T(8,128)(2,1)} async-done(((bf16[4,1024,768]{2,1,0:T(8,128)(2,1)}), bf16[4,128,768]{2,1,0:T(8,128)(2,1)}) %reduce-scatter.7.cloned.1.call-update) | async-done | bytes 786448 | tf_op jit(solution)/shard_map/reduce_scatter | solution.py:229
  932.2 6.0 fusion.64
  938.2 27.1 %all-reduce.17 = (bf16[768]{0:T(1024)(128)(2,1)S(1)}, bf16[768]{0:T(1024)(128)(2,1)S(1)}, bf16[768]{0:T(1024)(128)(2,1)S(1)}, bf16[768]{0:T(1024)(128)(2,1)S(1)}...) all-reduce(bf16[768]{0:T(1024)(128)(2,1)S(1)} %dynamic-update-slice, ...), channel_id=1, replica_groups=mesh['dp'=4,'fsdp'=8] {'fsdp'}, use_global_device_ids=true, to_apply=%add.7 | all-reduce | flops 9984 | bytes 39936
  966.0 12.3 all-reduce.19
  988.1 99.8 %reduce-scatter.15.cloned.1.call-done = bf16[96,3072]{1,0:T(8,128)(2,1)} async-done(((bf16[768,3072]{1,0:T(8,128)(2,1)}), bf16[96,3072]{1,0:T(8,128)(2,1)}) %reduce-scatter.15.cloned.1.call-update) | async-done | bytes 589840 | tf_op jit(solution)/shard_map/reduce_scatter | solution.py:285
  1087.9 98.7 %reduce-scatter.17.cloned.1.call-done = bf16[384,768]{1,0:T(8,128)(2,1)} async-done(((bf16[3072,768]{1,0:T(8,128)(2,1)}), bf16[384,768]{1,0:T(8,128)(2,1)}) %reduce-scatter.17.cloned.1.call-update) | async-done | bytes 589840 | tf_op jit(solution)/shard_map/reduce_scatter | solution.py:291
  1186.6 82.4 %reduce-scatter.11.cloned.1.call-done = bf16[96,2304]{1,0:T(8,128)(2,1)} async-done(((bf16[768,2304]{1,0:T(8,128)(2,1)}), bf16[96,2304]{1,0:T(8,128)(2,1)}) %reduce-scatter.11.cloned.1.call-update) | async-done | bytes 442384 | tf_op jit(solution)/shard_map/reduce_scatter | solution.py:264
  1269.1 9.0 add_convert_fusion
  1278.1 39.7 %all-reduce.23.cloned.1.call-done = (bf16[96,2304]{1,0:T(8,128)(2,1)}, bf16[96,768]{1,0:T(8,128)(2,1)}, bf16[96,3072]{1,0:T(8,128)(2,1)}, bf16[384,768]{1,0:T(8,128)(2,1)}) async-done(((bf16[96,2304]{1,0:T(8,128)(2,1)}, bf16[96,768]{1,0:T(8,128)(2,1)}, bf16[96,3072]{1,0:T(8,128)(2,1)}, bf16[384,768]{1,0:T(8,128)(2,1)}), (bf16[96,2304]{1,0:T(8,128)(2,1)}, bf16[96,768]{1,0:T(8,128)(2,1)}, ...) | async-done | bytes 1769488 | tf_op jit(solution)/shard_map/psum | solution.py:305
  (530 shorter events, 317.4 us)
Async XLA Ops:
  7.2 37.8 %copy-start.2 = (bf16[4,128,768]{2,1,0:T(8,128)(2,1)S(1)}, bf16[4,128,768]{2,1,0:T(8,128)(2,1)}, u32[]{:S(2)}) copy-start(bf16[4,128,768]{2,1,0:T(8,128)(2,1)} %param.24) | copy-start | bytes 2359300
  7.2 68.3 %all-gather.8.cloned.1.call-start = ((), (), s32[]{:S(2)}) async-start(), calls=%async_computation.6 | async-start | bytes 3981312 | tf_op jit(solution)/shard_map/all_gather | solution.py:127
  7.9 173.3 %all-gather.10.cloned.1.call-start = ((), (), s32[]{:S(2)}) async-start(), calls=%async_computation.7 | async-start | bytes 7077888 | tf_op jit(solution)/shard_map/all_gather | solution.py:148
  46.3 33.1 %copy-start.11 = (bf16[512,768]{1,0:T(8,128)(2,1)}, bf16[512,768]{1,0:T(8,128)(2,1)S(1)}, u32[]{:S(2)}) copy-start(bf16[512,768]{1,0:T(8,128)(2,1)S(1)} %fusion.58) | copy-start | bytes 2359300
  82.8 199.0 %all-gather.12.cloned.1.call-start = ((), (), s32[]{:S(2)}) async-start(), calls=%async_computation.8 | async-start | bytes 7077888 | tf_op jit(solution)/shard_map/all_gather | solution.py:149
  85.1 3.0 copy-start.23
  85.1 24.8 %copy-start.22 = (s32[4,128]{1,0:T(4,128)S(1)}, s32[4,128]{1,0:T(4,128)}, u32[]{:S(2)}) copy-start(s32[4,128]{1,0:T(4,128)} %param.25) | copy-start | bytes 6148
  86.3 264.3 %all-gather.14.cloned.1.call-start = ((), (), s32[]{:S(2)}) async-start(), calls=%async_computation.9 | async-start | bytes 1327104 | tf_op jit(solution)/shard_map/all_gather | solution.py:128
  86.8 317.5 %all-gather.16.cloned.1.call-start = ((), (), s32[]{:S(2)}) async-start(), calls=%async_computation.10 | async-start | bytes 5308416 | tf_op jit(solution)/shard_map/all_gather | solution.py:167
  87.4 397.0 %all-gather.18.cloned.1.call-start = ((), (), s32[]{:S(2)}) async-start(), calls=%async_computation.11 | async-start | bytes 5308416 | tf_op jit(solution)/shard_map/all_gather | solution.py:168
  88.0 713.3 %reduce-scatter.9.cloned.1.call-start = ((), (), s32[]{:S(2)}) async-start(), calls=%async_computation.13 | async-start | bytes 7077888 | tf_op jit(solution)/shard_map/reduce_scatter | solution.py:232
  353.2 143.5 %copy-start.4 = (f32[512,768]{1,0:T(8,128)}, f32[512,768]{1,0:T(8,128)S(1)}, u32[]{:S(2)}) copy-start(f32[512,768]{1,0:T(8,128)S(1)} %get-tuple-element.380) | copy-start | bytes 4718596
  353.5 130.9 %copy-start.9 = (bf16[4,128,768]{2,1,0:T(8,128)(2,1)S(1)}, bf16[4,128,768]{2,1,0:T(8,128)(2,1)}, u32[]{:S(2)}) copy-start(bf16[4,128,768]{2,1,0:T(8,128)(2,1)} %param.26) | copy-start | bytes 2359300
  484.4 9.2 copy-start.24
  493.6 3.0 copy-start.27
  497.3 2.3 copy-start
  683.9 238.1 %reduce-scatter.7.cloned.1.call-start = ((), (), s32[]{:S(2)}) async-start(), calls=%async_computation.12 | async-start | bytes 7077888 | tf_op jit(solution)/shard_map/reduce_scatter | solution.py:229
  684.7 3.7 copy-start.5
  684.7 303.4 %reduce-scatter.13.cloned.1.call-start = ((), (), s32[]{:S(2)}) async-start(), calls=%async_computation.15 | async-start | bytes 1327104 | tf_op jit(solution)/shard_map/reduce_scatter | solution.py:273
  688.4 399.5 %reduce-scatter.15.cloned.1.call-start = ((), (), s32[]{:S(2)}) async-start(), calls=%async_computation.16 | async-start | bytes 5308416 | tf_op jit(solution)/shard_map/reduce_scatter | solution.py:285
  695.0 491.6 %reduce-scatter.17.cloned.1.call-start = ((), (), s32[]{:S(2)}) async-start(), calls=%async_computation.17 | async-start | bytes 5308416 | tf_op jit(solution)/shard_map/reduce_scatter | solution.py:291
  704.8 217.3 %copy-start.12 = (bf16[512,768]{1,0:T(8,128)(2,1)S(1)}, bf16[512,768]{1,0:T(8,128)(2,1)}, u32[]{:S(2)}) copy-start(bf16[512,768]{1,0:T(8,128)(2,1)} %copy-done.11) | copy-start | bytes 2359300
  704.8 564.2 %reduce-scatter.11.cloned.1.call-start = ((), (), s32[]{:S(2)}) async-start(), calls=%async_computation.14 | async-start | bytes 3981312 | tf_op jit(solution)/shard_map/reduce_scatter | solution.py:264
  927.5 4.7 copy-start.3
  927.5 4.7 copy-start.17
  927.5 4.7 copy-start.19
  927.5 4.7 copy-start.21
  927.5 390.3 %all-reduce.23.cloned.1.call-start = ((), (), s32[]{:S(2)}) async-start(), calls=%async_computation.18 | async-start | bytes 3538944 | tf_op jit(solution)/shard_map/psum | solution.py:305
  929.1 3.1 copy-start.13
  985.8 283.3 %copy-start.6 = (f32[512,768]{1,0:T(8,128)S(1)}, f32[512,768]{1,0:T(8,128)}, u32[]{:S(2)}) copy-start(f32[512,768]{1,0:T(8,128)} %copy-done.4) | copy-start | bytes 4718596
  1317.8 3.8 copy-start.15
  1319.5 3.2 copy-start.14
  (12 other events, 17.6 us)
Sparse Core Ops, SparseCore 0:
  10.2 65.1 all-gather.7
  83.0 98.1 all-gather.9
  183.8 98.0 all-gather.11
  283.9 40.1 all-gather.13
  326.1 78.1 all-gather.15
  406.4 78.0 all-gather.17
  684.1 117.1 reduce-scatter.8
  804.9 117.1 reduce-scatter.6
  926.0 62.0 reduce-scatter.12
  991.6 96.2 reduce-scatter.14
  1091.6 94.9 reduce-scatter.16
  1190.1 78.9 reduce-scatter.10
  1271.6 46.0 all-reduce.22
where the time goes:
time: 1340 us; the launch traced here: 1330 us
  waiting for transfers between devices  843 us (63%)
  matrix products  229 us (17%)
  blocking collectives  111 us (8%)
  local copies, waits for them, and re-layouts  94.1 us (7%)
  other arithmetic  34.3 us (3%)
  between operations  16.4 us (1%)
    reduce_scatter x1, waiting for transfers between devices, local(): lax.psum_scatter(d_key_all.astype(jnp.bfloat16), 'fsdp', scatter_dimensio...  121 us
    all_gather x1, waiting for transfers between devices, local(): lax.all_gather(value_seq, 'fsdp', axis=1, tiled=True)  101 us
    reduce_scatter x1, waiting for transfers between devices, local(): lax.psum_scatter(partial_grads[7].astype(jnp.bfloat16), 'fsdp', scatter_d...  99.8 us
    reduce_scatter x1, waiting for transfers between devices, local(): lax.psum_scatter(partial_grads[9].astype(jnp.bfloat16), 'fsdp', scatter_d...  98.7 us
    reduce_scatter x1, waiting for transfers between devices, local(): lax.psum_scatter(d_value_all.astype(jnp.bfloat16), 'fsdp', scatter_dimens...  96.4 us
    reduce_scatter x1, waiting for transfers between devices, local(): lax.psum_scatter(partial_grads[0].astype(jnp.bfloat16), 'fsdp', scatter_d...  82.4 us
    all_gather x1, waiting for transfers between devices, local(): lax.all_gather(mlp_local[1], 'fsdp', axis=0, tiled=True)  73 us
    unnamed x2, blocking collectives  54.8 us
  transfers between devices with their start and end apart: 13, of which 12 were waited for; matrix products, arithmetic and copies ran while one was open for 11% of the time, Pallas kernels for 0%

commit v1 on v0

v1 whole, which is shorter than its diff:
```python
import jax
import jax.numpy as jnp
from jax import lax
from jax.experimental import pallas as pl
from jax.experimental.pallas import tpu as pltpu
from jax.sharding import PartitionSpec as P

HEAD_DIM = 64
NEG = -1e30
f32 = jnp.float32
bf16 = jnp.bfloat16


def dot(a, b, ca, cb):
    return lax.dot_general(a, b, (((ca,), (cb,)), ((), ())), preferred_element_type=f32)


def block_scores(k, q_block, seg_col, seg_row, start, rows):
    parts = []
    if start:
        s = dot(k[:start], q_block, 1, 1)
        parts.append(jnp.where(seg_col[:start] == seg_row, s, NEG))
    s = dot(k[start : start + rows], q_block, 1, 1)
    row = lax.broadcasted_iota(jnp.int32, s.shape, 0)
    col = lax.broadcasted_iota(jnp.int32, s.shape, 1)
    parts.append(jnp.where((seg_col[start : start + rows] == seg_row) & (row <= col), s, NEG))
    return parts


def attend_kernel(q_ref, k_ref, v_ref, seg_col_ref, seg_row_ref, o_ref, lse_ref, *, rows):
    length = k_ref.shape[0]
    for head in range(2):
        lanes = slice(head * HEAD_DIM, (head + 1) * HEAD_DIM)
        k = k_ref[:, lanes]
        v_t = v_ref[:, lanes].T
        for start in range(0, length, rows):
            stop = start + rows
            parts = block_scores(
                k, q_ref[start:stop, lanes], seg_col_ref, seg_row_ref[:, start:stop], start, rows
            )
            top = jnp.max(parts[-1], axis=0, keepdims=True)
            if start:
                top = jnp.maximum(top, jnp.max(parts[0], axis=0, keepdims=True))
            expo = [jnp.exp(s - top) for s in parts]
            total = sum(jnp.sum(e, axis=0, keepdims=True) for e in expo)
            mixed = dot(v_t[:, start:stop], expo[-1].astype(bf16), 1, 0)
            if start:
                mixed += dot(v_t[:, :start], expo[0].astype(bf16), 1, 0)
            o_ref[start:stop, lanes] = (mixed / total).T.astype(bf16)
            lse_ref[head : head + 1, start:stop] = top + jnp.log(total)


def attend_back_kernel(
    q_ref, k_ref, v_ref, do_ref, lse_ref, seg_col_ref, seg_row_ref, dq_ref, dk_ref, dv_ref, dk_acc, dv_acc, *, rows
):
    length = k_ref.shape[0]
    scale = HEAD_DIM ** (-0.5)
    for head in range(2):
        lanes = slice(head * HEAD_DIM, (head + 1) * HEAD_DIM)
        k = k_ref[:, lanes]
        v = v_ref[:, lanes]
        k_t = k.T
        for start in range(length - rows, -1, -rows):
            stop = start + rows
            q_block = q_ref[start:stop, lanes]
            do_block = do_ref[start:stop, lanes]
            lse = lse_ref[head : head + 1, start:stop]
            parts = block_scores(k, q_block, seg_col_ref, seg_row_ref[:, start:stop], start, rows)
            spans = [(0, start), (start, stop)] if start else [(start, stop)]
            probs = [jnp.exp(s - lse) for s in parts]
            d_probs = [dot(v[lo:hi], do_block, 1, 1) for lo, hi in spans]
            delta = sum(jnp.sum(p * d, axis=0, keepdims=True) for p, d in zip(probs, d_probs))
            dq_t = 0.0
            for (lo, hi), p, d in zip(spans, probs, d_probs):
                ds = (p * (d - delta)).astype(bf16)
                dq_t += dot(k_t[:, lo:hi], ds, 1, 0)
                dk_part = dot(ds, q_block, 1, 0)
                dv_part = dot(p.astype(bf16), do_block, 1, 0)
                if stop == length:
                    dk_acc[lo:hi, :] = dk_part
                    dv_acc[lo:hi, :] = dv_part
                else:
                    dk_acc[lo:hi, :] += dk_part
                    dv_acc[lo:hi, :] += dv_part
            dq_ref[start:stop, lanes] = (dq_t * scale).T.astype(bf16)
        dk_ref[:, lanes] = dk_acc[...].astype(bf16)
        dv_ref[:, lanes] = dv_acc[...].astype(bf16)


def attend(q, k, v, seg_col, seg_row):
    length, width = q.shape
    pairs = width // 128
    wide = pl.BlockSpec((length, 128), lambda p: (0, p))
    return pl.pallas_call(
        lambda *refs: attend_kernel(*refs, rows=min(256, length)),
        out_shape=(
            jax.ShapeDtypeStruct((length, width), bf16),
            jax.ShapeDtypeStruct((pairs, 8, length), f32),
        ),
        grid=(pairs,),
        in_specs=[
            wide,
            wide,
            wide,
            pl.BlockSpec((length, 1), lambda p: (0, 0)),
            pl.BlockSpec((1, length), lambda p: (0, 0)),
        ],
        out_specs=(wide, pl.BlockSpec((None, 8, length), lambda p: (p, 0, 0))),
        compiler_params=pltpu.CompilerParams(vmem_limit_bytes=48 * 1024 * 1024),
        cost_estimate=pl.CostEstimate(
            flops=4 * length * length * width, bytes_accessed=8 * length * width, transcendentals=length * length * 4
        ),
        name="attend",
    )(q, k, v, seg_col, seg_row)


def attend_back(q, k, v, d_mixed, lse, seg_col, seg_row):
    length, width = q.shape
    pairs = width // 128
    wide = pl.BlockSpec((length, 128), lambda p: (0, p))
    return pl.pallas_call(
        lambda *refs: attend_back_kernel(*refs, rows=min(256, length)),
        out_shape=(jax.ShapeDtypeStruct((length, width), bf16),) * 3,
        grid=(pairs,),
        in_specs=[
            wide,
            wide,
            wide,
            wide,
            pl.BlockSpec((None, 8, length), lambda p: (p, 0, 0)),
            pl.BlockSpec((length, 1), lambda p: (0, 0)),
            pl.BlockSpec((1, length), lambda p: (0, 0)),
        ],
        out_specs=(wide, wide, wide),
        scratch_shapes=[pltpu.VMEM((length, HEAD_DIM), f32)] * 2,
        compiler_params=pltpu.CompilerParams(vmem_limit_bytes=48 * 1024 * 1024),
        cost_estimate=pl.CostEstimate(
            flops=10 * length * length * width, bytes_accessed=16 * length * width, transcendentals=length * length * 4
        ),
        name="attend_back",
    )(q, k, v, d_mixed, lse, seg_col, seg_row)


def split_heads(t):
    return t.reshape(t.shape[0], -1, HEAD_DIM).transpose(1, 0, 2)


def join_heads(t):
    return t.transpose(1, 0, 2).reshape(t.shape[1], -1)


def attend_far(q, k, v, allowed):
    def one(item):
        qh, kh, vh = item
        s = jnp.where(allowed, dot(qh, kh, 1, 1), NEG)
        top = jnp.max(s, axis=-1, keepdims=True)
        e = jnp.exp(s - top)
        total = jnp.sum(e, axis=-1, keepdims=True)
        return dot((e / total).astype(bf16), vh, 1, 0), (top + jnp.log(total))[:, 0]

    mixed, lse = lax.map(one, (split_heads(q), split_heads(k), split_heads(v)))
    return join_heads(mixed).astype(bf16), lse


def attend_far_back(q, k, v, d_mixed, lse, allowed):
    def one(item):
        qh, kh, vh, dh, l = item
        p = jnp.exp(jnp.where(allowed, dot(qh, kh, 1, 1), NEG) - l[:, None])
        dp = dot(dh, vh, 1, 1)
        ds = (p * (dp - jnp.sum(p * dp, axis=-1, keepdims=True))).astype(bf16)
        return (
            dot(ds, kh, 1, 0) * HEAD_DIM ** (-0.5),
            dot(ds, qh, 0, 0),
            dot(p.astype(bf16), dh, 0, 0),
        )

    grads = lax.map(one, (split_heads(q), split_heads(k), split_heads(v), split_heads(d_mixed), lse))
    return tuple(join_heads(g) for g in grads)


def standardize(values):
    centered = values - jnp.mean(values, axis=-1, keepdims=True)
    spread = jnp.mean(centered * centered, axis=-1, keepdims=True)
    inverse = lax.rsqrt(spread + 1e-05)
    return centered * inverse, inverse


def norm_backward(grad, xhat, inverse, gain):
    dz = grad * gain
    d_in = inverse * (
        dz - jnp.mean(dz, axis=-1, keepdims=True) - xhat * jnp.mean(dz * xhat, axis=-1, keepdims=True)
    )
    return d_in, jnp.sum(grad * xhat, axis=0), jnp.sum(grad, axis=0)


def build(dp_size, fsdp_size):
    F = fsdp_size
    X = dp_size // 2
    inner = 2 ** ((F.bit_length() - 1) // 2)
    outer = F // inner

    def swap(a):
        return lax.ppermute(a, "dp", [(d, d ^ 1) for d in range(dp_size)])

    def along(a, step_outer, step_inner):
        perm = []
        for o in range(outer):
            for i in range(inner):
                src = ((o + step_outer) % outer) * inner + (i + step_inner) % inner
                perm.append((src, o * inner + i))
        return lax.ppermute(a, "fsdp", perm)

    def gather(a, o, i):
        line = jnp.zeros((outer,) + a.shape, a.dtype)
        for step in range(outer):
            piece = along(a, step, 0) if step else a
            line = lax.dynamic_update_index_in_dim(line, piece, (o + step) % outer, 0)
        if inner == 2:
            other = along(line, 0, 1)
            first = i == 0
            both = jnp.stack([jnp.where(first, line, other), jnp.where(first, other, line)], axis=1)
        else:
            both = jnp.zeros((outer, inner) + a.shape, a.dtype)
            for step in range(inner):
                piece = along(line, 0, step) if step else line
                both = lax.dynamic_update_index_in_dim(both, piece, (i + step) % inner, 1)
        return both.reshape((F,) + a.shape)

    def reduce(a, o, i):
        a = a.reshape((outer, inner) + a.shape[1:])
        total = lax.dynamic_index_in_dim(a, i, 1, keepdims=False).astype(f32)
        for step in range(1, inner):
            total += along(
                lax.dynamic_index_in_dim(a, (i + inner - step) % inner, 1, keepdims=False), 0, step
            ).astype(f32)
        a = total.astype(bf16)
        total = lax.dynamic_index_in_dim(a, o, 0, keepdims=False).astype(f32)
        for step in range(1, outer):
            total += along(
                lax.dynamic_index_in_dim(a, (o + outer - step) % outer, 0, keepdims=False), step, 0
            ).astype(f32)
        a = total.astype(bf16)
        total = a.astype(f32)
        for step in range(1, X):
            total += lax.ppermute(
                a, "dp", [(d, (d + 2 * step) % dp_size) for d in range(dp_size)]
            ).astype(f32)
        return total.astype(bf16)

    def local(
        inputs,
        segments,
        cotangent,
        qkv_weight,
        query_bias,
        value_bias,
        out_weight,
        out_bias,
        norm1_gain,
        norm1_shift,
        up_weight,
        up_bias,
        down_weight,
        down_bias,
        norm2_gain,
        norm2_shift,
    ):
        seqs, block, width = inputs.shape
        hidden = up_weight.shape[1]
        chips = F // (2 * seqs)
        per_core = F // chips // 2
        own = per_core * block
        half = width // 2
        part = width // F
        deep = hidden // F
        core = lax.axis_index("dp") % 2
        f = lax.axis_index("fsdp")
        o, i = f // inner, f % inner
        is_first = core == 0

        def route(k, back):
            perm = []
            for x in range(X):
                for c in range(2):
                    for b in range(F):
                        t = b % per_core
                        to_core = (b // per_core) % 2
                        to_chip = (c * seqs + (t ^ k)) * chips + b // (2 * per_core)
                        pair = ((x * 2 + c) * F + b, (x * 2 + to_core) * F + to_chip)
                        perm.append(pair[::-1] if back else pair)
            return perm

        slot = f % per_core
        seq_here = (f // chips) % seqs

        def to_chips(a):
            got = [
                lax.ppermute(
                    lax.dynamic_index_in_dim(a, slot ^ k, 0, keepdims=False), ("dp", "fsdp"), route(k, False)
                )
                for k in range(seqs)
            ]
            got = jnp.stack(got)
            return jnp.concatenate(
                [lax.dynamic_index_in_dim(got, t ^ seq_here, 0) for t in range(per_core)], axis=0
            )

        def to_blocks(a):
            a = a.reshape(per_core, block, width)
            got = [
                lax.ppermute(
                    lax.dynamic_index_in_dim(a, seq_here ^ k, 0, keepdims=False), ("dp", "fsdp"), route(k, True)
                )
                for k in range(seqs)
            ]
            got = jnp.stack(got)
            return jnp.concatenate(
                [lax.dynamic_index_in_dim(got, s ^ slot, 0) for s in range(seqs)], axis=0
            )

        def in_order(mine, other, axis):
            return jnp.concatenate(
                [jnp.where(is_first, mine, other), jnp.where(is_first, other, mine)], axis=axis
            )

        small = jnp.concatenate(
            [query_bias, value_bias, out_bias, norm1_gain, norm1_shift, down_bias, norm2_gain, norm2_shift, up_bias]
        )
        heads_w = jnp.concatenate(
            [lax.dynamic_slice_in_dim(qkv_weight, n * width + core * half, half, 1) for n in range(3)], axis=1
        )
        lanes = heads_w.shape[1]
        first_pack = jnp.concatenate(
            [heads_w, jnp.pad(small[None], ((0, 7), (0, lanes - small.shape[0])))], axis=0
        )
        first_all = gather(first_pack, o, i)
        w_heads = first_all[:, :part].reshape(width, lanes)
        small_all = first_all[:, part].astype(f32)
        vectors = small_all[:, : 8 * part].reshape(F, 8, part).transpose(1, 0, 2).reshape(8, width)
        b_query, b_value, b_out, gain1, shift1, b_down, gain2, shift2 = [vectors[n] for n in range(8)]
        b_up_all = small_all[:, 8 * part : 8 * part + deep].reshape(F, 2, deep // 2)

        seg_row_own = jnp.pad(segments.astype(bf16)[:, None, :], ((0, 0), (0, 7), (0, width - block)))
        tokens = to_chips(jnp.concatenate([inputs, seg_row_own], axis=1))
        tokens_other = swap(tokens)
        grad_low = to_chips(cotangent).reshape(own, width)

        up_half = lax.dynamic_index_in_dim(
            up_weight.reshape(part, F, 2, deep // 2), core, 2, keepdims=False
        ).reshape(part, hidden // 2)
        out_half = lax.dynamic_slice_in_dim(out_weight, core * half, half, 1)
        down_half = lax.dynamic_slice_in_dim(down_weight, core * (deep // 2), deep // 2, 0)
        second_all = gather(jnp.concatenate([up_half, out_half], axis=1), o, i).reshape(width, -1)
        second_other = swap(second_all)
        third_all = gather(down_half, o, i).reshape(hidden // 2, width)
        third_other = swap(third_all)
        ups = (second_all[:, : hidden // 2], second_other[:, : hidden // 2])
        downs = (third_all, third_other)
        w_out = in_order(second_all[:, hidden // 2 :], second_other[:, hidden // 2 :], 1)

        x_own = tokens[:, :block].reshape(own, width).astype(f32)
        x_all = in_order(
            tokens[:, :block].reshape(own, width), tokens_other[:, :block].reshape(own, width), 0
        ).astype(f32)
        xhat_all, _ = standardize(x_all)
        hidden1 = (xhat_all * gain1 + shift1).astype(bf16)
        seg = in_order(
            tokens[:, block, :block].reshape(own), tokens_other[:, block, :block].reshape(own), 0
        ).astype(f32)
        joined = jnp.dot(hidden1, w_heads, preferred_element_type=f32)
        bq = lax.dynamic_slice_in_dim(b_query, core * half, half)
        bv = lax.dynamic_slice_in_dim(b_value, core * half, half)
        q = (joined[:, :half] + bq).astype(bf16) * bf16(HEAD_DIM ** (-0.5))
        k = joined[:, half : 2 * half].astype(bf16)
        v = (joined[:, 2 * half :] + bv).astype(bf16)
        if chips == 1:
            seg_col, seg_row = seg[:, None], seg[None, :]
            mixed, lse = attend(q, k, v, seg_col, seg_row)
        else:
            groups = [[g * chips + n for n in range(chips)] for g in range(F // chips)]
            k, v, seg_keys = (
                lax.all_gather(t, "fsdp", axis=0, tiled=True, axis_index_groups=groups) for t in (k, v, seg)
            )
            position = (f % chips) * 2 * own + jnp.arange(2 * own, dtype=jnp.int32)
            allowed = (jnp.arange(k.shape[0], dtype=jnp.int32)[None, :] <= position[:, None]) & (
                seg_keys[None, :] == seg[:, None]
            )
            mixed, lse = attend_far(q, k, v, allowed)

        mixed_other = swap(lax.dynamic_slice_in_dim(mixed, (1 - core) * own, own, 0))
        mixed_own = in_order(lax.dynamic_slice_in_dim(mixed, core * own, own, 0), mixed_other, 1)
        midway = x_own + jnp.dot(mixed_own, w_out, preferred_element_type=f32) + b_out
        xhat2, inverse2 = standardize(midway)
        hidden2 = (xhat2 * gain2 + shift2).astype(bf16)
        pre_acts, activs, pulls = [], [], []
        result = midway + b_down
        for n in range(2):
            b_up = lax.dynamic_index_in_dim(b_up_all, core ^ n, 1, keepdims=False).reshape(hidden // 2)
            pre = jnp.dot(hidden2, ups[n], preferred_element_type=f32) + b_up
            act, pull = jax.vjp(lambda t: jax.nn.gelu(t, approximate=True), pre)
            act = act.astype(bf16)
            activs.append(act)
            pulls.append(pull)
            result += jnp.dot(act, downs[n], preferred_element_type=f32)
        output = to_blocks(result.astype(bf16))

        grad_out = grad_low.astype(f32)
        d_down_b = jnp.sum(grad_out, axis=0)
        d_pres = [None, None]
        d_downs = [None, None]
        d_ups = [None, None]
        for n in (1, 0):
            d_downs[n] = dot(activs[n], grad_low, 0, 0).astype(bf16)
            d_pres[n] = pulls[n](dot(grad_low, downs[n], 1, 1))[0].astype(bf16)
            d_ups[n] = dot(hidden2, d_pres[n], 0, 0).astype(bf16)
        d_down_sum = (d_downs[0].astype(f32) + swap(d_downs[1]).astype(f32)).astype(bf16)
        d_down_red = reduce(d_down_sum.reshape(F, deep // 2, width), o, i)
        d_hidden2 = dot(d_pres[0], ups[0], 1, 1) + dot(d_pres[1], ups[1], 1, 1)
        d_up_bs = [jnp.sum(t.astype(f32), axis=0) for t in d_pres]
        d_norm2, d_gain2, d_shift2 = norm_backward(d_hidden2, xhat2, inverse2, gain2)
        d_mid = grad_out + d_norm2
        d_branch = d_mid.astype(bf16)
        d_mixed = dot(d_branch, w_out, 1, 1).astype(bf16)
        d_mixed_other = swap(lax.dynamic_slice_in_dim(d_mixed, (1 - core) * half, half, 1))
        d_out = dot(mixed_own, d_branch, 0, 0).astype(bf16)
        d_out_b = jnp.sum(d_branch.astype(f32), axis=0)
        give = jnp.concatenate([d_ups[1], lax.dynamic_slice_in_dim(d_out, (1 - core) * half, half, 1)], axis=1)
        keep = jnp.concatenate([d_ups[0], lax.dynamic_slice_in_dim(d_out, core * half, half, 1)], axis=1)
        d_second = (keep.astype(f32) + swap(give).astype(f32)).astype(bf16)
        d_second_red = reduce(d_second.reshape(F, part, -1), o, i)

        d_heads = in_order(lax.dynamic_slice_in_dim(d_mixed, core * half, half, 1), d_mixed_other, 0)
        if chips == 1:
            dq, dk, dv = attend_back(q, k, v, d_heads, lse, seg_col, seg_row)
        else:
            dq, dk, dv = attend_far_back(q, k, v, d_heads, lse, allowed)
            dk, dv = (
                lax.psum_scatter(
                    t.astype(bf16), "fsdp", scatter_dimension=0, tiled=True, axis_index_groups=groups
                )
                for t in (dk, dv)
            )
            dq = dq.astype(bf16)
        d_joined = jnp.concatenate([dq, dk, dv], axis=1)
        d_hidden1 = dot(d_joined, w_heads, 1, 1)
        d_hidden1_other = swap(lax.dynamic_slice_in_dim(d_hidden1, (1 - core) * own, own, 0).astype(bf16))
        d_hidden1 = lax.dynamic_slice_in_dim(d_hidden1, core * own, own, 0) + d_hidden1_other.astype(f32)
        xhat1, inverse1 = standardize(x_own)
        d_norm1, d_gain1, d_shift1 = norm_backward(d_hidden1, xhat1, inverse1, gain1)
        d_inputs = to_blocks((d_mid + d_norm1).astype(bf16))

        d_w_heads = dot(hidden1, d_joined, 0, 0)
        d_bias = jnp.sum(d_joined.astype(f32), axis=0)

        def placed(vector):
            return lax.dynamic_update_slice_in_dim(jnp.zeros((width,), f32), vector, core * half, 0)

        d_vectors = jnp.stack(
            [placed(d_bias[:half]), placed(d_bias[2 * half :]), d_out_b, d_gain1, d_shift1, d_down_b, d_gain2, d_shift2]
        )
        d_vectors = d_vectors.reshape(8, F, part).transpose(1, 0, 2).reshape(F, 8 * part)
        d_up_b = in_order(d_up_bs[0].reshape(F, 1, deep // 2), d_up_bs[1].reshape(F, 1, deep // 2), 1)
        d_small = jnp.concatenate([d_vectors, d_up_b.reshape(F, deep)], axis=1)
        d_small = jnp.pad(d_small[:, None], ((0, 0), (0, 7), (0, lanes - d_small.shape[1])))
        d_first = jnp.concatenate([d_w_heads.reshape(F, part, lanes), d_small], axis=1).astype(bf16)
        d_first_red = reduce(d_first, o, i)

        first_o = swap(d_first_red)
        second_o = swap(d_second_red)
        down_o = swap(d_down_red)
        cols = half
        pieces = []
        for n in range(3):
            sl = slice(n * cols, (n + 1) * cols)
            pieces.append(in_order(d_first_red[:part, sl], first_o[:part, sl], 1))
        d_qkv_w = jnp.concatenate(pieces, axis=1).astype(f32)
        small_sum = d_first_red[part].astype(f32) + first_o[part].astype(f32)
        vec = [small_sum[n * part : (n + 1) * part] for n in range(8)]
        d_up_b = small_sum[8 * part : 8 * part + deep]
        up_m = d_second_red[:, : hidden // 2].reshape(part, F, 1, deep // 2)
        up_o = second_o[:, : hidden // 2].reshape(part, F, 1, deep // 2)
        d_up_w = in_order(up_m, up_o, 2).reshape(part, hidden).astype(f32)
        d_out_w = in_order(d_second_red[:, hidden // 2 :], second_o[:, hidden // 2 :], 1).astype(f32)
        d_down_w = in_order(d_down_red, down_o, 0).astype(f32)
        return (
            output,
            d_inputs,
            d_qkv_w,
            vec[0],
            vec[1],
            d_out_w,
            vec[2],
            vec[3],
            vec[4],
            d_up_w,
            d_up_b,
            d_down_w,
            vec[5],
            vec[6],
            vec[7],
        )

    return local


def solution(mesh):
    in_specs = (
        P("dp", "fsdp", None),
        P("dp", "fsdp"),
        P("dp", "fsdp", None),
        P("fsdp", None),
        P("fsdp"),
        P("fsdp"),
        P("fsdp", None),
        P("fsdp"),
        P("fsdp"),
        P("fsdp"),
        P("fsdp", None),
        P("fsdp"),
        P("fsdp", None),
        P("fsdp"),
        P("fsdp"),
        P("fsdp"),
    )
    out_specs = (
        P("dp", "fsdp", None),
        P("dp", "fsdp", None),
        P("fsdp", None),
        P("fsdp"),
        P("fsdp"),
        P("fsdp", None),
        P("fsdp"),
        P("fsdp"),
        P("fsdp"),
        P("fsdp", None),
        P("fsdp"),
        P("fsdp", None),
        P("fsdp"),
        P("fsdp"),
        P("fsdp"),
    )
    local = build(mesh.shape["dp"], mesh.shape["fsdp"])
    return jax.shard_map(local, mesh=mesh, in_specs=in_specs, out_specs=out_specs, check_vma=False)
```

time: 1340 us -> 506 us (0.38)
  waiting for transfers between devices: 843 us -> 237 us
  matrix products: 229 us -> 62.3 us
  blocking collectives: 111 us -> 0 us
  starting transfers between devices: 0.52 us -> 91.1 us
  local copies, waits for them, and re-layouts: 94.1 us -> 36.1 us
  Pallas kernels: 0 us -> 27.8 us
  between operations: 16.4 us -> 2.64 us
    reduce_scatter x6 -> x0, waiting for transfers between devices: 500 us -> none  [the longest x1 121 us: local(): lax.psum_scatter(d_key_all.astype(jnp.bfloat16), 'fsdp', scatter_dimensio...]
    all_gather x6 -> x0, waiting for transfers between devices: 300 us -> none  [the longest x1 101 us: local(): lax.all_gather(value_seq, 'fsdp', axis=1, tiled=True)]
    ppermute x0 -> x54, waiting for transfers between devices: none -> 237 us  [the longest x24 197 us: along(): return lax.ppermute(a, 'fsdp', perm)]
    dot_general x180 -> x18, matrix products: 229 us -> 62.3 us  [the longest x12 46.4 us: dot(): lax.dot_general(a, b, (((ca,), (cb,)), ((), ())), preferred_element_type=...]
    ppermute x0 -> x54, starting transfers between devices: none -> 91.1 us  [the longest x24 33.9 us: along(): return lax.ppermute(a, 'fsdp', perm)]
    unnamed x2 -> x0, blocking collectives: 54.8 us -> none
    all_gather x2 -> x0, blocking collectives: 44.1 us -> none  [the longest x1 22.4 us: local(): all_segs = lax.all_gather(segments, 'fsdp', axis=1, tiled=True)]
    psum x1 -> x0, waiting for transfers between devices: 39.7 us -> none  [local(): lax.psum(shards[0].astype(jnp.bfloat16), 'dp').astype(jnp.float32)]
  transfers between devices with their start and end apart: 13 -> 54, of which waited for: 12 -> 25; matrix products, arithmetic and copies ran while one was open for 11% -> 18% of each run, Pallas kernels for 0% -> 6%
where the time goes in v1:
time: 506 us; the launch traced here: 499 us
  waiting for transfers between devices  237 us (47%)
  starting transfers between devices  91.1 us (18%)
  matrix products  62.3 us (12%)
  other arithmetic  42.8 us (8%)
  local copies, waits for them, and re-layouts  36.1 us (7%)
  Pallas kernels  27.8 us (5%)
    ppermute x24, waiting for transfers between devices, along(): return lax.ppermute(a, 'fsdp', perm)  197 us
    dot_general x12, matrix products, dot(): lax.dot_general(a, b, (((ca,), (cb,)), ((), ())), preferred_element_type=...  46.4 us
    ppermute x24, starting transfers between devices, along(): return lax.ppermute(a, 'fsdp', perm)  33.9 us
    ppermute x8, starting transfers between devices, to_chips(): lax.ppermute(lax.dynamic_index_in_dim(a, slot ^ k, 0, keepdims=False), ('...  23.1 us
    ppermute x8, starting transfers between devices, to_blocks(): lax.ppermute(lax.dynamic_index_in_dim(a, seq_here ^ k, 0, keepdims=False)...  18.3 us
    pallas_call x1, Pallas kernels, attend_back(): pl.pallas_call(lambda *refs: attend_back_kernel(*refs, rows=min(256, leng...  17.7 us
    ppermute x8, waiting for transfers between devices, to_blocks(): lax.ppermute(lax.dynamic_index_in_dim(a, seq_here ^ k, 0, keepdims=False)...  16.2 us
    ppermute x8, waiting for transfers between devices, to_chips(): lax.ppermute(lax.dynamic_index_in_dim(a, slot ^ k, 0, keepdims=False), ('...  14.2 us
  transfers between devices with their start and end apart: 54, of which 25 were waited for; matrix products, arithmetic and copies ran while one was open for 18% of the time, Pallas kernels for 6%

profile of v1, /device:TPU:9, one launch (start us, length us, event | category | flops | bytes accessed | tf_op | source)
XLA Modules:
  0.0 499.4 jit_solution(18413186969356632998)
XLA Ops:
  7.9 4.5 collective-permute-start.25
  29.1 4.6 collective-permute-start.1
  33.7 5.2 %collective-permute-start = (bf16[136,768]{1,0:T(8,128)(2,1)}, bf16[136,768]{1,0:T(8,128)(2,1)}, u32[]{:S(2)}, u32[]{:S(2)}) collective-permute-start(bf16[136,768]{1,0:T(8,128)(2,1)} %get-tuple-element.94), channel_id=1, source_target_pairs={{0,0},{1,1},{2,2},{3,3},{4,8},{5,9},{6,10},{7,11},{8,4},{9,5},{10,... | collective-permute-start | bytes 626696 | tf_op jit(solution)/shard_map/ppermute | solution.py:298
  42.0 5.0 %collective-permute-done.3 = bf16[136,768]{1,0:T(8,128)(2,1)} collective-permute-done((bf16[136,768]{1,0:T(8,128)(2,1)}, bf16[136,768]{1,0:T(8,128)(2,1)}, u32[]{:S(2)}, u32[]{:S(2)}) %collective-permute-start.3) | collective-permute-done | bytes 208928 | tf_op jit(solution)/shard_map/ppermute | solution.py:298
  53.0 10.5 %collective-permute-start.5 = (bf16[104,1152]{1,0:T(8,128)(2,1)}, bf16[104,1152]{1,0:T(8,128)(2,1)S(1)}, u32[]{:S(2)}, u32[]{:S(2)}) collective-permute-start(bf16[104,1152]{1,0:T(8,128)(2,1)} %fusion.64), channel_id=1, source_target_pairs={{2,0},{3,1},{4,2},{5,3},{6,4},{7,5},{0,6},{1,7},{10,8},{11,9},{12,... | collective-permute-start | bytes 718856 | tf_op jit(solution)/shard_map/ppermute | solution.py:211
  65.6 5.3 %collective-permute-done.5 = bf16[104,1152]{1,0:T(8,128)(2,1)S(1)} collective-permute-done((bf16[104,1152]{1,0:T(8,128)(2,1)}, bf16[104,1152]{1,0:T(8,128)(2,1)S(1)}, u32[]{:S(2)}, u32[]{:S(2)}) %collective-permute-start.5) | collective-permute-done | bytes 239648 | tf_op jit(solution)/shard_map/ppermute | solution.py:211
  70.8 4.6 collective-permute-start.7
  76.2 6.9 %collective-permute-done.6 = bf16[104,1152]{1,0:T(8,128)(2,1)S(1)} collective-permute-done((bf16[104,1152]{1,0:T(8,128)(2,1)}, bf16[104,1152]{1,0:T(8,128)(2,1)S(1)}, u32[]{:S(2)}, u32[]{:S(2)}) %collective-permute-start.6) | collective-permute-done | bytes 239648 | tf_op jit(solution)/shard_map/ppermute | solution.py:211
  90.5 5.6 %collective-permute-start.4 = (bf16[4,136,768]{2,1,0:T(8,128)(2,1)S(1)}, bf16[4,136,768]{2,1,0:T(8,128)(2,1)S(1)}, u32[]{:S(2)}, u32[]{:S(2)}) collective-permute-start(bf16[4,136,768]{2,1,0:T(8,128)(2,1)S(1)} %pad_maximum_fusion.7), channel_id=1, source_target_pairs={{0,8},{8,0},{16,24},{24,16},{1,9},{9,1},{17,25},{25,17},{2,10},{10... | collective-permute-start | bytes 2506760 | tf_op jit(solution)/shard_map/ppermute | solution.py:203
  99.1 11.2 %collective-permute-done.11 = bf16[96,1920]{1,0:T(8,128)(2,1)S(1)} collective-permute-done((bf16[96,1920]{1,0:T(8,128)(2,1)S(1)}, bf16[96,1920]{1,0:T(8,128)(2,1)S(1)}, u32[]{:S(2)}, u32[]{:S(2)}) %collective-permute-start.11) | collective-permute-done | bytes 368672 | tf_op jit(solution)/shard_map/ppermute | solution.py:211
  110.3 7.9 %collective-permute-done.12 = bf16[96,1920]{1,0:T(8,128)(2,1)S(1)} collective-permute-done((bf16[96,1920]{1,0:T(8,128)(2,1)S(1)}, bf16[96,1920]{1,0:T(8,128)(2,1)S(1)}, u32[]{:S(2)}, u32[]{:S(2)}) %collective-permute-start.12) | collective-permute-done | bytes 368672 | tf_op jit(solution)/shard_map/ppermute | solution.py:211
  124.5 52.4 %collective-permute-done.13 = bf16[4,96,1920]{2,1,0:T(8,128)(2,1)} collective-permute-done((bf16[4,96,1920]{2,1,0:T(8,128)(2,1)S(1)}, bf16[4,96,1920]{2,1,0:T(8,128)(2,1)}, u32[]{:S(2)}, u32[]{:S(2)}) %collective-permute-start.13) | collective-permute-done | bytes 1474592 | tf_op jit(solution)/shard_map/ppermute | solution.py:211
  183.5 3.9 fusion.76
  188.7 10.1 %attend.1 = (bf16[1024,384]{1,0:T(8,128)(2,1)S(1)}, f32[3,8,1024]{2,1,0:T(8,128)S(1)}) custom-call(bf16[1024,384]{1,0:T(8,128)(2,1)S(1)} %get-tuple-element.63.refs_0_, bf16[1024,384]{1,0:T(8,128)(2,1)S(1)} %get-tuple-element.62.refs_1_, bf16[1024,384]{1,0:T(8,128)(2,1)S(1)} %fusion.30.refs_2_, f32[1024,1]{1,0:T(8,128)S(1)} %copy-done.2, ...), custom_call_target="tpu_custom_call" | custom-call | flops 1610612736 | bytes 3145728 | tf_op jit(solution)/shard_map/attend/pallas_call | solution.py:94
  209.9 4.2 convolution_add_fusion
  219.2 14.8 %convert_reduce_fusion.2 = (bf16[1536]{0:T(1024)(128)(2,1)S(1)}, bf16[512,1536]{1,0:T(8,128)(2,1)S(1)}) fusion(f32[512,1536]{1,0:T(8,128)S(1)} %convolution_add_fusion, bf16[512,768]{1,0:T(8,128)(2,1)S(1)} %bitcast.250, bf16[1536,768]{1,0:T(8,128)(2,1)S(1)} %collective-permute-done.19), kind=kOutput, calls=%fused_computation.36 | convolution fusion | flops 1225259520 | bytes 7867392 | tf_op jit(solution)/shard_map/dot_general | solution.py:15
  258.8 4.6 collective-permute-start.21
  280.5 17.7 %attend_back.1 = (bf16[1024,384]{1,0:T(8,128)(2,1)S(1)}, bf16[1024,384]{1,0:T(8,128)(2,1)S(1)}, bf16[1024,384]{1,0:T(8,128)(2,1)S(1)}) custom-call(bf16[1024,384]{1,0:T(8,128)(2,1)S(1)} %get-tuple-element.63.refs_0_, bf16[1024,384]{1,0:T(8,128)(2,1)S(1)} %get-tuple-element.62.refs_1_, bf16[1024,384]{1,0:T(8,128)(2,1)S(1)} %fusion.30.refs_2_, ...), custom_call_target="tpu_custom_call" | custom-call | flops 4026531840 | bytes 6291456 | tf_op jit(solution)/shard_map/attend_back/pallas_call | solution.py:121
  304.9 4.6 convolution_convert_fusion.4
  309.5 3.6 fusion.44
  317.4 22.7 %collective-permute-done.34 = bf16[4,104,1152]{2,1,0:T(8,128)(2,1)S(1)} collective-permute-done((bf16[4,104,1152]{2,1,0:T(8,128)(2,1)S(1)}, bf16[4,104,1152]{2,1,0:T(8,128)(2,1)S(1)}, u32[]{:S(2)}, u32[]{:S(2)}) %collective-permute-start.34) | collective-permute-done | bytes 958496 | tf_op jit(solution)/shard_map/ppermute | solution.py:211
  340.1 4.6 collective-permute-start.31
  348.8 10.0 %collective-permute-done.30 = bf16[128,768]{1,0:T(8,128)(2,1)S(1)} collective-permute-done((bf16[128,768]{1,0:T(8,128)(2,1)S(1)}, bf16[128,768]{1,0:T(8,128)(2,1)S(1)}, u32[]{:S(2)}, u32[]{:S(2)}) %collective-permute-start.30) | collective-permute-done | bytes 196640 | tf_op jit(solution)/shard_map/ppermute | solution.py:311
  358.8 5.2 %collective-permute-start.35 = (bf16[104,1152]{1,0:T(8,128)(2,1)S(1)}, bf16[104,1152]{1,0:T(8,128)(2,1)S(1)}, u32[]{:S(2)}, u32[]{:S(2)}) collective-permute-start(bf16[104,1152]{1,0:T(8,128)(2,1)S(1)} %get-tuple-element.86), channel_id=1, source_target_pairs={{2,0},{3,1},{4,2},{5,3},{6,4},{7,5},{0,6},{1,7},{10,8},{11,9},{12,... | collective-permute-start | bytes 718856 | tf_op jit(solution)/shard_map/ppermute | solution.py:211
  365.2 6.9 %collective-permute-done.36 = bf16[104,1152]{1,0:T(8,128)(2,1)S(1)} collective-permute-done((bf16[104,1152]{1,0:T(8,128)(2,1)S(1)}, bf16[104,1152]{1,0:T(8,128)(2,1)S(1)}, u32[]{:S(2)}, u32[]{:S(2)}) %collective-permute-start.36) | collective-permute-done | bytes 239648 | tf_op jit(solution)/shard_map/ppermute | solution.py:211
  375.4 3.8 collective-permute-done.38
  381.5 3.7 add_convert_fusion.1
  390.0 22.9 %collective-permute-done.48 = bf16[4,192,768]{2,1,0:T(8,128)(2,1)S(1)} collective-permute-done((bf16[4,192,768]{2,1,0:T(8,128)(2,1)S(1)}, bf16[4,192,768]{2,1,0:T(8,128)(2,1)S(1)}, u32[]{:S(2)}, u32[]{:S(2)}) %collective-permute-start.48) | collective-permute-done | bytes 1179680 | tf_op jit(solution)/shard_map/ppermute | solution.py:211
  415.1 29.5 %collective-permute-done.41 = bf16[4,96,1920]{2,1,0:T(8,128)(2,1)S(1)} collective-permute-done((bf16[4,96,1920]{2,1,0:T(8,128)(2,1)S(1)}, bf16[4,96,1920]{2,1,0:T(8,128)(2,1)S(1)}, u32[]{:S(2)}, u32[]{:S(2)}) %collective-permute-start.41) | collective-permute-done | bytes 1474592 | tf_op jit(solution)/shard_map/ppermute | solution.py:211
  448.0 6.3 %collective-permute-done.44 = bf16[96,1920]{1,0:T(8,128)(2,1)S(1)} collective-permute-done((bf16[96,1920]{1,0:T(8,128)(2,1)S(1)}, bf16[96,1920]{1,0:T(8,128)(2,1)S(1)}, u32[]{:S(2)}, u32[]{:S(2)}) %collective-permute-start.44) | collective-permute-done | bytes 368672 | tf_op jit(solution)/shard_map/ppermute | solution.py:211
  454.4 21.8 %collective-permute-done.43 = bf16[96,1920]{1,0:T(8,128)(2,1)S(1)} collective-permute-done((bf16[96,1920]{1,0:T(8,128)(2,1)S(1)}, bf16[96,1920]{1,0:T(8,128)(2,1)S(1)}, u32[]{:S(2)}, u32[]{:S(2)}) %collective-permute-start.43) | collective-permute-done | bytes 368672 | tf_op jit(solution)/shard_map/ppermute | solution.py:211
  482.5 5.4 %collective-permute-done.45 = bf16[96,1920]{1,0:T(8,128)(2,1)S(1)} collective-permute-done((bf16[96,1920]{1,0:T(8,128)(2,1)S(1)}, bf16[96,1920]{1,0:T(8,128)(2,1)S(1)}, u32[]{:S(2)}, u32[]{:S(2)}) %collective-permute-start.45) | collective-permute-done | bytes 368672 | tf_op jit(solution)/shard_map/ppermute | solution.py:245
  (367 shorter events, 167.0 us)
Async XLA Ops:
  3.7 83.5 %collective-permute-start.15 = (bf16[192,768]{1,0:T(8,128)(2,1)S(1)}, bf16[192,768]{1,0:T(8,128)(2,1)S(1)}, u32[]{:S(2)}, u32[]{:S(2)}) collective-permute-start(bf16[192,768]{1,0:T(8,128)(2,1)S(1)} %get-tuple-element.59), channel_id=1, source_target_pairs={{2,0},{3,1},{4,2},{5,3},{6,4},{7,5},{0,6},{1,7},{10,8},{11,9},{12,... | collective-permute-start | bytes 884744 | tf_op jit(solution)/shard_map/ppermute | solution.py:211
  7.9 21.2 %collective-permute-start.25 = (bf16[128,768]{1,0:T(8,128)(2,1)}, bf16[128,768]{1,0:T(8,128)(2,1)}, u32[]{:S(2)}, u32[]{:S(2)}) collective-permute-start(bf16[128,768]{1,0:T(8,128)(2,1)} %get-tuple-element.113), channel_id=1, source_target_pairs={{0,1},{1,0},{2,3},{3,2},{4,9},{5,8},{6,11},{7,10},{8,5},{9,4},{10,... | collective-permute-start | bytes 589832 | tf_op jit(solution)/shard_map/ppermute | solution.py:298
  12.4 21.3 %collective-permute-start.24 = (bf16[128,768]{1,0:T(8,128)(2,1)}, bf16[128,768]{1,0:T(8,128)(2,1)}, u32[]{:S(2)}, u32[]{:S(2)}) collective-permute-start(bf16[128,768]{1,0:T(8,128)(2,1)} %get-tuple-element.112), channel_id=1, source_target_pairs={{0,0},{1,1},{2,2},{3,3},{4,8},{5,9},{6,10},{7,11},{8,4},{9,5},{10,... | collective-permute-start | bytes 589832 | tf_op jit(solution)/shard_map/ppermute | solution.py:298
  22.2 24.7 %collective-permute-start.3 = (bf16[136,768]{1,0:T(8,128)(2,1)}, bf16[136,768]{1,0:T(8,128)(2,1)}, u32[]{:S(2)}, u32[]{:S(2)}) collective-permute-start(bf16[136,768]{1,0:T(8,128)(2,1)} %get-tuple-element.95), channel_id=1, source_target_pairs={{0,3},{1,2},{2,1},{3,0},{4,11},{5,10},{6,9},{7,8},{8,7},{9,6},{10,... | collective-permute-start | bytes 626696 | tf_op jit(solution)/shard_map/ppermute | solution.py:298
  24.8 25.7 %collective-permute-start.2 = (bf16[136,768]{1,0:T(8,128)(2,1)}, bf16[136,768]{1,0:T(8,128)(2,1)}, u32[]{:S(2)}, u32[]{:S(2)}) collective-permute-start(bf16[136,768]{1,0:T(8,128)(2,1)} %get-tuple-element.96), channel_id=1, source_target_pairs={{0,2},{1,3},{2,0},{3,1},{4,10},{5,11},{6,8},{7,9},{8,6},{9,7},{10,... | collective-permute-start | bytes 626696 | tf_op jit(solution)/shard_map/ppermute | solution.py:298
  29.1 23.9 %collective-permute-start.1 = (bf16[136,768]{1,0:T(8,128)(2,1)}, bf16[136,768]{1,0:T(8,128)(2,1)}, u32[]{:S(2)}, u32[]{:S(2)}) collective-permute-start(bf16[136,768]{1,0:T(8,128)(2,1)} %get-tuple-element.97), channel_id=1, source_target_pairs={{0,1},{1,0},{2,3},{3,2},{4,9},{5,8},{6,11},{7,10},{8,5},{9,4},{10,... | collective-permute-start | bytes 626696 | tf_op jit(solution)/shard_map/ppermute | solution.py:298
  33.7 29.7 %collective-permute-start = (bf16[136,768]{1,0:T(8,128)(2,1)}, bf16[136,768]{1,0:T(8,128)(2,1)}, u32[]{:S(2)}, u32[]{:S(2)}) collective-permute-start(bf16[136,768]{1,0:T(8,128)(2,1)} %get-tuple-element.94), channel_id=1, source_target_pairs={{0,0},{1,1},{2,2},{3,3},{4,8},{5,9},{6,10},{7,11},{8,4},{9,5},{10,... | collective-permute-start | bytes 626696 | tf_op jit(solution)/shard_map/ppermute | solution.py:298
  47.0 43.6 %collective-permute-start.16 = (bf16[192,768]{1,0:T(8,128)(2,1)S(1)}, bf16[192,768]{1,0:T(8,128)(2,1)S(1)}, u32[]{:S(2)}, u32[]{:S(2)}) collective-permute-start(bf16[192,768]{1,0:T(8,128)(2,1)S(1)} %get-tuple-element.59), channel_id=1, source_target_pairs={{4,0},{5,1},{6,2},{7,3},{0,4},{1,5},{2,6},{3,7},{12,8},{13,9},{14,... | collective-permute-start | bytes 884744 | tf_op jit(solution)/shard_map/ppermute | solution.py:211
  50.5 46.3 %collective-permute-start.17 = (bf16[192,768]{1,0:T(8,128)(2,1)S(1)}, bf16[192,768]{1,0:T(8,128)(2,1)S(1)}, u32[]{:S(2)}, u32[]{:S(2)}) collective-permute-start(bf16[192,768]{1,0:T(8,128)(2,1)S(1)} %get-tuple-element.59), channel_id=1, source_target_pairs={{6,0},{7,1},{0,2},{1,3},{2,4},{3,5},{4,6},{5,7},{14,8},{15,9},{8,1... | collective-permute-start | bytes 884744 | tf_op jit(solution)/shard_map/ppermute | solution.py:211
  63.4 19.7 %collective-permute-start.6 = (bf16[104,1152]{1,0:T(8,128)(2,1)}, bf16[104,1152]{1,0:T(8,128)(2,1)S(1)}, u32[]{:S(2)}, u32[]{:S(2)}) collective-permute-start(bf16[104,1152]{1,0:T(8,128)(2,1)} %fusion.64), channel_id=1, source_target_pairs={{4,0},{5,1},{6,2},{7,3},{0,4},{1,5},{2,6},{3,7},{12,8},{13,9},{14,... | collective-permute-start | bytes 718856 | tf_op jit(solution)/shard_map/ppermute | solution.py:211
  85.6 24.7 %collective-permute-start.11 = (bf16[96,1920]{1,0:T(8,128)(2,1)S(1)}, bf16[96,1920]{1,0:T(8,128)(2,1)S(1)}, u32[]{:S(2)}, u32[]{:S(2)}) collective-permute-start(bf16[96,1920]{1,0:T(8,128)(2,1)S(1)} %pad_maximum_fusion.20), channel_id=1, source_target_pairs={{4,0},{5,1},{6,2},{7,3},{0,4},{1,5},{2,6},{3,7},{12,8},{13,9},{14,... | collective-permute-start | bytes 1105928 | tf_op jit(solution)/shard_map/ppermute | solution.py:211
  87.2 30.9 %collective-permute-start.12 = (bf16[96,1920]{1,0:T(8,128)(2,1)S(1)}, bf16[96,1920]{1,0:T(8,128)(2,1)S(1)}, u32[]{:S(2)}, u32[]{:S(2)}) collective-permute-start(bf16[96,1920]{1,0:T(8,128)(2,1)S(1)} %pad_maximum_fusion.20), channel_id=1, source_target_pairs={{6,0},{7,1},{0,2},{1,3},{2,4},{3,5},{4,6},{5,7},{14,8},{15,9},{8,1... | collective-permute-start | bytes 1105928 | tf_op jit(solution)/shard_map/ppermute | solution.py:211
  90.5 29.0 %collective-permute-start.4 = (bf16[4,136,768]{2,1,0:T(8,128)(2,1)S(1)}, bf16[4,136,768]{2,1,0:T(8,128)(2,1)S(1)}, u32[]{:S(2)}, u32[]{:S(2)}) collective-permute-start(bf16[4,136,768]{2,1,0:T(8,128)(2,1)S(1)} %pad_maximum_fusion.7), channel_id=1, source_target_pairs={{0,8},{8,0},{16,24},{24,16},{1,9},{9,1},{17,25},{25,17},{2,10},{10... | collective-permute-start | bytes 2506760 | tf_op jit(solution)/shard_map/ppermute | solution.py:203
  96.8 26.0 %collective-permute-start.8 = (bf16[4,104,1152]{2,1,0:T(8,128)(2,1)}, bf16[4,104,1152]{2,1,0:T(8,128)(2,1)}, u32[]{:S(2)}, u32[]{:S(2)}) collective-permute-start(bf16[4,104,1152]{2,1,0:T(8,128)(2,1)} %bitcast_dynamic-update-slice_fusion.8), channel_id=1, source_target_pairs={{1,0},{0,1},{3,2},{2,3},{5,4},{4,5},{7,6},{6,7},{9,8},{8,9},{11,10... | collective-permute-start | bytes 2875400 | tf_op jit(solution)/shard_map/ppermute | solution.py:211
  99.0 101.2 %collective-permute-start.18 = (bf16[4,192,768]{2,1,0:T(8,128)(2,1)}, bf16[4,192,768]{2,1,0:T(8,128)(2,1)}, u32[]{:S(2)}, u32[]{:S(2)}) collective-permute-start(bf16[4,192,768]{2,1,0:T(8,128)(2,1)} %bitcast_dynamic-update-slice_fusion.4), channel_id=1, source_target_pairs={{1,0},{0,1},{3,2},{2,3},{5,4},{4,5},{7,6},{6,7},{9,8},{8,9},{11,10... | collective-permute-start | bytes 3538952 | tf_op jit(solution)/shard_map/ppermute | solution.py:211
  118.2 58.7 %collective-permute-start.13 = (bf16[4,96,1920]{2,1,0:T(8,128)(2,1)S(1)}, bf16[4,96,1920]{2,1,0:T(8,128)(2,1)}, u32[]{:S(2)}, u32[]{:S(2)}) collective-permute-start(bf16[4,96,1920]{2,1,0:T(8,128)(2,1)S(1)} %bitcast_dynamic-update-slice_fusion), channel_id=1, source_target_pairs={{1,0},{0,1},{3,2},{2,3},{5,4},{4,5},{7,6},{6,7},{9,8},{8,9},{11,10... | collective-permute-start | bytes 4423688 | tf_op jit(solution)/shard_map/ppermute | solution.py:211
  180.4 23.5 %collective-permute-start.14 = (bf16[768,1920]{1,0:T(8,128)(2,1)}, bf16[768,1920]{1,0:T(8,128)(2,1)}, u32[]{:S(2)}, u32[]{:S(2)}) collective-permute-start(bf16[768,1920]{1,0:T(8,128)(2,1)} %bitcast.33), channel_id=1, source_target_pairs={{0,8},{8,0},{16,24},{24,16},{1,9},{9,1},{17,25},{25,17},{2,10},{10... | collective-permute-start | bytes 8847368 | tf_op jit(solution)/shard_map/ppermute | solution.py:203
  271.1 115.3 %collective-permute-start.40 = (bf16[768,1920]{1,0:T(8,128)(2,1)}, bf16[768,1920]{1,0:T(8,128)(2,1)}, u32[]{:S(2)}, u32[]{:S(2)}) collective-permute-start(bf16[768,1920]{1,0:T(8,128)(2,1)} %pad_maximum_fusion.1), channel_id=1, source_target_pairs={{0,8},{8,0},{16,24},{24,16},{1,9},{9,1},{17,25},{25,17},{2,10},{10... | collective-permute-start | bytes 8847368 | tf_op jit(solution)/shard_map/ppermute | solution.py:203
  271.6 109.9 %collective-permute-start.47 = (bf16[1536,768]{1,0:T(8,128)(2,1)}, bf16[1536,768]{1,0:T(8,128)(2,1)}, u32[]{:S(2)}, u32[]{:S(2)}) collective-permute-start(bf16[1536,768]{1,0:T(8,128)(2,1)} %convolution_convert_fusion), channel_id=1, source_target_pairs={{0,8},{8,0},{16,24},{24,16},{1,9},{9,1},{17,25},{25,17},{2,10},{10... | collective-permute-start | bytes 7077896 | tf_op jit(solution)/shard_map/ppermute | solution.py:203
  313.6 26.6 %collective-permute-start.34 = (bf16[4,104,1152]{2,1,0:T(8,128)(2,1)S(1)}, bf16[4,104,1152]{2,1,0:T(8,128)(2,1)S(1)}, u32[]{:S(2)}, u32[]{:S(2)}) collective-permute-start(bf16[4,104,1152]{2,1,0:T(8,128)(2,1)S(1)} %fusion.49), channel_id=1, source_target_pairs={{1,0},{0,1},{3,2},{2,3},{5,4},{4,5},{7,6},{6,7},{9,8},{8,9},{11,10... | collective-permute-start | bytes 2875400 | tf_op jit(solution)/shard_map/ppermute | solution.py:211
  316.0 28.9 %collective-permute-start.33 = (bf16[128,768]{1,0:T(8,128)(2,1)S(1)}, bf16[128,768]{1,0:T(8,128)(2,1)S(1)}, u32[]{:S(2)}, u32[]{:S(2)}) collective-permute-start(bf16[128,768]{1,0:T(8,128)(2,1)S(1)} %get-tuple-element.103), channel_id=1, source_target_pairs={{3,0},{2,1},{1,2},{0,3},{11,4},{10,5},{9,6},{8,7},{7,8},{6,9},{5,1... | collective-permute-start | bytes 589832 | tf_op jit(solution)/shard_map/ppermute | solution.py:311
  316.2 31.0 %collective-permute-start.32 = (bf16[128,768]{1,0:T(8,128)(2,1)S(1)}, bf16[128,768]{1,0:T(8,128)(2,1)S(1)}, u32[]{:S(2)}, u32[]{:S(2)}) collective-permute-start(bf16[128,768]{1,0:T(8,128)(2,1)S(1)} %get-tuple-element.104), channel_id=1, source_target_pairs={{2,0},{3,1},{0,2},{1,3},{10,4},{11,5},{8,6},{9,7},{6,8},{7,9},{4,1... | collective-permute-start | bytes 589832 | tf_op jit(solution)/shard_map/ppermute | solution.py:311
  347.2 18.0 %collective-permute-start.37 = (bf16[104,1152]{1,0:T(8,128)(2,1)S(1)}, bf16[104,1152]{1,0:T(8,128)(2,1)S(1)}, u32[]{:S(2)}, u32[]{:S(2)}) collective-permute-start(bf16[104,1152]{1,0:T(8,128)(2,1)S(1)} %get-tuple-element.87), channel_id=1, source_target_pairs={{6,0},{7,1},{0,2},{1,3},{2,4},{3,5},{4,6},{5,7},{14,8},{15,9},{8,1... | collective-permute-start | bytes 718856 | tf_op jit(solution)/shard_map/ppermute | solution.py:211
  348.2 23.9 %collective-permute-start.36 = (bf16[104,1152]{1,0:T(8,128)(2,1)S(1)}, bf16[104,1152]{1,0:T(8,128)(2,1)S(1)}, u32[]{:S(2)}, u32[]{:S(2)}) collective-permute-start(bf16[104,1152]{1,0:T(8,128)(2,1)S(1)} %get-tuple-element.88), channel_id=1, source_target_pairs={{4,0},{5,1},{6,2},{7,3},{0,4},{1,5},{2,6},{3,7},{12,8},{13,9},{14,... | collective-permute-start | bytes 718856 | tf_op jit(solution)/shard_map/ppermute | solution.py:211
  385.3 27.6 %collective-permute-start.48 = (bf16[4,192,768]{2,1,0:T(8,128)(2,1)S(1)}, bf16[4,192,768]{2,1,0:T(8,128)(2,1)S(1)}, u32[]{:S(2)}, u32[]{:S(2)}) collective-permute-start(bf16[4,192,768]{2,1,0:T(8,128)(2,1)S(1)} %dynamic-slice_bitcast_fusion.1), channel_id=1, source_target_pairs={{1,0},{0,1},{3,2},{2,3},{5,4},{4,5},{7,6},{6,7},{9,8},{8,9},{11,10... | collective-permute-start | bytes 3538952 | tf_op jit(solution)/shard_map/ppermute | solution.py:211
  389.1 55.5 %collective-permute-start.41 = (bf16[4,96,1920]{2,1,0:T(8,128)(2,1)S(1)}, bf16[4,96,1920]{2,1,0:T(8,128)(2,1)S(1)}, u32[]{:S(2)}, u32[]{:S(2)}) collective-permute-start(bf16[4,96,1920]{2,1,0:T(8,128)(2,1)S(1)} %dynamic-slice_bitcast_fusion), channel_id=1, source_target_pairs={{1,0},{0,1},{3,2},{2,3},{5,4},{4,5},{7,6},{6,7},{9,8},{8,9},{11,10... | collective-permute-start | bytes 4423688 | tf_op jit(solution)/shard_map/ppermute | solution.py:211
  413.3 31.9 %collective-permute-start.51 = (bf16[192,768]{1,0:T(8,128)(2,1)S(1)}, bf16[192,768]{1,0:T(8,128)(2,1)S(1)}, u32[]{:S(2)}, u32[]{:S(2)}) collective-permute-start(bf16[192,768]{1,0:T(8,128)(2,1)S(1)} %get-tuple-element.78), channel_id=1, source_target_pairs={{6,0},{7,1},{0,2},{1,3},{2,4},{3,5},{4,6},{5,7},{14,8},{15,9},{8,1... | collective-permute-start | bytes 884744 | tf_op jit(solution)/shard_map/ppermute | solution.py:211
  413.6 33.0 %collective-permute-start.50 = (bf16[192,768]{1,0:T(8,128)(2,1)S(1)}, bf16[192,768]{1,0:T(8,128)(2,1)S(1)}, u32[]{:S(2)}, u32[]{:S(2)}) collective-permute-start(bf16[192,768]{1,0:T(8,128)(2,1)S(1)} %get-tuple-element.79), channel_id=1, source_target_pairs={{4,0},{5,1},{6,2},{7,3},{0,4},{1,5},{2,6},{3,7},{12,8},{13,9},{14,... | collective-permute-start | bytes 884744 | tf_op jit(solution)/shard_map/ppermute | solution.py:211
  413.7 32.9 %collective-permute-start.49 = (bf16[192,768]{1,0:T(8,128)(2,1)S(1)}, bf16[192,768]{1,0:T(8,128)(2,1)S(1)}, u32[]{:S(2)}, u32[]{:S(2)}) collective-permute-start(bf16[192,768]{1,0:T(8,128)(2,1)S(1)} %get-tuple-element.77), channel_id=1, source_target_pairs={{2,0},{3,1},{4,2},{5,3},{6,4},{7,5},{0,6},{1,7},{10,8},{11,9},{12,... | collective-permute-start | bytes 884744 | tf_op jit(solution)/shard_map/ppermute | solution.py:211
  445.1 31.1 %collective-permute-start.43 = (bf16[96,1920]{1,0:T(8,128)(2,1)S(1)}, bf16[96,1920]{1,0:T(8,128)(2,1)S(1)}, u32[]{:S(2)}, u32[]{:S(2)}) collective-permute-start(bf16[96,1920]{1,0:T(8,128)(2,1)S(1)} %get-tuple-element.76), channel_id=1, source_target_pairs={{4,0},{5,1},{6,2},{7,3},{0,4},{1,5},{2,6},{3,7},{12,8},{13,9},{14,... | collective-permute-start | bytes 1105928 | tf_op jit(solution)/shard_map/ppermute | solution.py:211
  445.2 32.8 %collective-permute-start.42 = (bf16[96,1920]{1,0:T(8,128)(2,1)S(1)}, bf16[96,1920]{1,0:T(8,128)(2,1)S(1)}, u32[]{:S(2)}, u32[]{:S(2)}) collective-permute-start(bf16[96,1920]{1,0:T(8,128)(2,1)S(1)} %get-tuple-element.74), channel_id=1, source_target_pairs={{2,0},{3,1},{4,2},{5,3},{6,4},{7,5},{0,6},{1,7},{10,8},{11,9},{12,... | collective-permute-start | bytes 1105928 | tf_op jit(solution)/shard_map/ppermute | solution.py:211
  446.8 34.9 %collective-permute-start.52 = (bf16[192,768]{1,0:T(8,128)(2,1)S(1)}, bf16[192,768]{1,0:T(8,128)(2,1)S(1)}, u32[]{:S(2)}, u32[]{:S(2)}) collective-permute-start(bf16[192,768]{1,0:T(8,128)(2,1)S(1)} %fusion.59), channel_id=1, source_target_pairs={{0,16},{8,24},{16,0},{24,8},{1,17},{9,25},{17,1},{25,9},{2,18},{10... | collective-permute-start | bytes 884744 | tf_op jit(solution)/shard_map/ppermute | solution.py:245
  (68 other events, 737.2 us)

commit v2 on v1

--- a/solution.py
+++ b/solution.py
@@ -7,6 +7,8 @@
 
 HEAD_DIM = 64
 NEG = -1e30
+GELU_A = 0.7978845608
+GELU_B = 0.044715
 f32 = jnp.float32
 bf16 = jnp.bfloat16
 
@@ -108,7 +110,7 @@
         out_specs=(wide, pl.BlockSpec((None, 8, length), lambda p: (p, 0, 0))),
         compiler_params=pltpu.CompilerParams(vmem_limit_bytes=48 * 1024 * 1024),
         cost_estimate=pl.CostEstimate(
-            flops=4 * length * length * width, bytes_accessed=8 * length * width, transcendentals=length * length * 4
+            flops=28 * length * length * width, bytes_accessed=8 * length * width, transcendentals=length * length * 4
         ),
         name="attend",
     )(q, k, v, seg_col, seg_row)
@@ -135,7 +137,7 @@
         scratch_shapes=[pltpu.VMEM((length, HEAD_DIM), f32)] * 2,
         compiler_params=pltpu.CompilerParams(vmem_limit_bytes=48 * 1024 * 1024),
         cost_estimate=pl.CostEstimate(
-            flops=10 * length * length * width, bytes_accessed=16 * length * width, transcendentals=length * length * 4
+            flops=50 * length * length * width, bytes_accessed=16 * length * width, transcendentals=length * length * 4
         ),
         name="attend_back",
     )(q, k, v, d_mixed, lse, seg_col, seg_row)
@@ -178,6 +180,130 @@
     return tuple(join_heads(g) for g in grads)
 
 
+def place(pieces, indices, shape, spans):
+    table = jnp.stack([jnp.asarray(v, jnp.int32) for index in indices for v in index])
+    offsets = []
+    for index in indices:
+        offsets.append(sum(len(t) for t in indices[: len(offsets)]))
+
+    def kernel(table_ref, *refs):
+        out_ref, sems = refs[len(pieces)], refs[len(pieces) + 1]
+        copies = []
+        for n, span in enumerate(spans):
+            spot = tuple(table_ref[offsets[n] + m] for m in range(len(indices[n])))
+            target = out_ref.at[spot] if span is None else out_ref.at[(span,) + spot]
+            copies.append(pltpu.make_async_copy(refs[n], target, sems.at[n]))
+        for copy in copies:
+            copy.start()
+        for copy in copies:
+            copy.wait()
+
+    size = 2
+    for extent in shape:
+        size *= extent
+    return pl.pallas_call(
+        kernel,
+        out_shape=jax.ShapeDtypeStruct(shape, pieces[0].dtype),
+        in_specs=[pl.BlockSpec(memory_space=pltpu.SMEM)] + [pl.BlockSpec(memory_space=pl.ANY)] * len(pieces),
+        out_specs=pl.BlockSpec(memory_space=pltpu.VMEM),
+        scratch_shapes=[pltpu.SemaphoreType.DMA((len(pieces),))],
+        compiler_params=pltpu.CompilerParams(vmem_limit_bytes=2 * size + (8 << 20)),
+        cost_estimate=pl.CostEstimate(flops=0, bytes_accessed=2 * size, transcendentals=0),
+        name="place",
+    )(table, *pieces)
+
+
+def after(a, *others):
+    return lax.optimization_barrier((a,) + others)[0] if others else a
+
+
+def row_pieces(deep):
+    pieces = []
+    for half in range(2):
+        at, stop = half * (deep // 2), (half + 1) * (deep // 2)
+        while at < stop:
+            end = min(stop, (at // 128 + 1) * 128)
+            pieces.append((half, at - half * (deep // 2), at // 128, at % 128, at % 128 + end - at))
+            at = end
+    return pieces
+
+
+def unpack_small(small, part, deep):
+    count = small.shape[0]
+
+    def kernel(in_ref, vec_ref, up_ref):
+        for f in range(count):
+            rows = in_ref[f].astype(f32)
+            vec_ref[:, f * part : (f + 1) * part] = rows[:8, :part]
+            for half, at, row, lo, hi in row_pieces(deep):
+                start = f * (deep // 2) + at
+                up_ref[half : half + 1, start : start + hi - lo] = rows[8 + row : 9 + row, lo:hi]
+
+    return pl.pallas_call(
+        kernel,
+        out_shape=(
+            jax.ShapeDtypeStruct((8, count * part), f32),
+            jax.ShapeDtypeStruct((2, count * (deep // 2)), f32),
+        ),
+        name="unpack_small",
+    )(small)
+
+
+def pack_small(core, rows_in, d_bias, d_up_mine, d_up_other, count, total_rows):
+    width = rows_in[0].shape[1]
+    part, half = width // count, width // 2
+    deep = 2 * d_up_mine.shape[1] // count
+    core = jnp.reshape(core, (1,)).astype(jnp.int32)
+
+    def kernel(core_ref, bias_ref, up_m_ref, up_o_ref, *refs):
+        out_ref, vec, up = refs[-3], refs[-2], refs[-1]
+        first = core_ref[0] == 0
+        none = jnp.zeros((1, half), f32)
+        for n, lo in enumerate((0, 2 * half)):
+            mine = bias_ref[:, lo : lo + half]
+            vec[n : n + 1, :half] = jnp.where(first, mine, none)
+            vec[n : n + 1, half:] = jnp.where(first, none, mine)
+        for n in range(6):
+            vec[2 + n : 3 + n, :] = refs[n][...]
+        up[0:1, :] = jnp.where(first, up_m_ref[...], up_o_ref[...])
+        up[1:2, :] = jnp.where(first, up_o_ref[...], up_m_ref[...])
+        out_ref[...] = jnp.zeros_like(out_ref)
+        for f in range(count):
+            out_ref[f, 0:8, :part] = vec[:, f * part : (f + 1) * part]
+            for which, at, row, lo, hi in row_pieces(deep):
+                start = f * (deep // 2) + at
+                out_ref[f, 8 + row : 9 + row, lo:hi] = up[which : which + 1, start : start + hi - lo]
+
+    return pl.pallas_call(
+        kernel,
+        out_shape=jax.ShapeDtypeStruct((count, total_rows, 128), f32),
+        in_specs=[pl.BlockSpec(memory_space=pltpu.SMEM)] + [pl.BlockSpec(memory_space=pltpu.VMEM)] * 9,
+        scratch_shapes=[pltpu.VMEM((8, width), f32), pltpu.VMEM((2, d_up_mine.shape[1]), f32)],
+        name="pack_small",
+    )(core, d_bias, d_up_mine, d_up_other, *rows_in)
+
+
+def weave(core, mine, other, count):
+    rows, cols = mine.shape
+    step = cols // count
+    core = jnp.reshape(core, (1,)).astype(jnp.int32)
+
+    def kernel(core_ref, mine_ref, other_ref, out_ref):
+        first = core_ref[0] == 0
+        a, b = mine_ref[...].astype(f32), other_ref[...].astype(f32)
+        low, high = jnp.where(first, a, b), jnp.where(first, b, a)
+        for n in range(count):
+            out_ref[:, 2 * n * step : (2 * n + 1) * step] = low[:, n * step : (n + 1) * step]
+            out_ref[:, (2 * n + 1) * step : (2 * n + 2) * step] = high[:, n * step : (n + 1) * step]
+
+    return pl.pallas_call(
+        kernel,
+        out_shape=jax.ShapeDtypeStruct((rows, 2 * cols), f32),
+        in_specs=[pl.BlockSpec(memory_space=pltpu.SMEM)] + [pl.BlockSpec(memory_space=pltpu.VMEM)] * 2,
+        name="weave",
+    )(core, mine, other)
+
+
 def standardize(values):
     centered = values - jnp.mean(values, axis=-1, keepdims=True)
     spread = jnp.mean(centered * centered, axis=-1, keepdims=True)
@@ -190,7 +316,7 @@
     d_in = inverse * (
         dz - jnp.mean(dz, axis=-1, keepdims=True) - xhat * jnp.mean(dz * xhat, axis=-1, keepdims=True)
     )
-    return d_in, jnp.sum(grad * xhat, axis=0), jnp.sum(grad, axis=0)
+    return d_in, jnp.sum(grad * xhat, axis=0, keepdims=True), jnp.sum(grad, axis=0, keepdims=True)
 
 
 def build(dp_size, fsdp_size):
@@ -210,42 +336,88 @@
                 perm.append((src, o * inner + i))
         return lax.ppermute(a, "fsdp", perm)
 
-    def gather(a, o, i):
-        line = jnp.zeros((outer,) + a.shape, a.dtype)
-        for step in range(outer):
-            piece = along(a, step, 0) if step else a
-            line = lax.dynamic_update_index_in_dim(line, piece, (o + step) % outer, 0)
-        if inner == 2:
-            other = along(line, 0, 1)
-            first = i == 0
-            both = jnp.stack([jnp.where(first, line, other), jnp.where(first, other, line)], axis=1)
-        else:
-            both = jnp.zeros((outer, inner) + a.shape, a.dtype)
-            for step in range(inner):
-                piece = along(line, 0, step) if step else line
-                both = lax.dynamic_update_index_in_dim(both, piece, (i + step) % inner, 1)
-        return both.reshape((F,) + a.shape)
-
-    def reduce(a, o, i):
-        a = a.reshape((outer, inner) + a.shape[1:])
-        total = lax.dynamic_index_in_dim(a, i, 1, keepdims=False).astype(f32)
+    def across(a, step):
+        return lax.ppermute(a, "dp", [((d + 2 * step) % dp_size, d) for d in range(dp_size)])
+
+    def gather_line(a, o, *late):
+        pieces = [after(a, *late)] + [along(a, step, 0) for step in range(1, outer)]
+        return place(
+            pieces, [((o + step) % outer,) for step in range(outer)], (outer,) + a.shape, [None] * outer
+        )
+
+    cube = inner == 2 and X == 2 and outer % 2 == 0
+    cut = outer // 2
+
+    def gather_sides(line):
+        return (across(line, 1), along(line, 0, 1)) if cube else ()
+
+    def gather_rest(line, sides, i, x):
+        shape = (outer, inner, X) + line.shape[1:]
+        if cube:
+            by_x, by_y = sides
+            low, high = across(by_y[:cut], 1), along(by_x[cut:], 0, 1)
+            return place(
+                [line, by_x, by_y, low, high],
+                [(i, x), (i, 1 - x), (1 - i, x), (1 - i, 1 - x), (1 - i, 1 - x)],
+                shape,
+                [slice(None)] * 3 + [slice(0, cut), slice(cut, outer)],
+            )
+        plane = jnp.zeros((outer, X) + line.shape[1:], line.dtype)
+        for step in range(X):
+            plane = lax.dynamic_update_index_in_dim(plane, across(line, step) if step else line, (x + step) % X, 1)
+        both = jnp.zeros(shape, line.dtype)
+        for step in range(inner):
+            both = lax.dynamic_update_index_in_dim(both, along(plane, 0, step) if step else plane, (i + step) % inner, 1)
+        return both
+
+    def pick(a, index, axis):
+        return lax.dynamic_index_in_dim(a, index, axis, keepdims=False)
+
+    def part(a, di, dx, i, x):
+        return pick(pick(a, i ^ di, 1), x ^ dx, 1)
+
+    def reduce_far(a, i, x):
+        if not cube:
+            return a, ()
+        far = part(a, 1, 1, i, x)
+        low, high = lax.optimization_barrier((far[:cut], far[cut:]))
+        return a, (along(low, 0, 1), across(high, 1))
+
+    def reduce_sides(state, i, x, late_far, late_sides):
+        a, far = state
+        if cube:
+            here = after(a, *late_far)
+            to_x, to_y = part(here, 0, 1, i, x), part(here, 1, 0, i, x)
+            from_y, from_x = far
+            to_x = jnp.concatenate([(to_x[:cut].astype(f32) + from_y.astype(f32)).astype(bf16), to_x[cut:]])
+            to_y = jnp.concatenate([to_y[:cut], (to_y[cut:].astype(f32) + from_x.astype(f32)).astype(bf16)])
+            to_x, to_y = lax.optimization_barrier((to_x, to_y))
+            own = part(after(a, *late_sides), 0, 0, i, x)
+            return (own.astype(f32) + across(to_x, 1).astype(f32) + along(to_y, 0, 1).astype(f32)).astype(bf16)
+        total = pick(a, x, 2).astype(f32)
+        for step in range(1, X):
+            total += across(pick(a, (x + X - step) % X, 2), step).astype(f32)
+        a = total.astype(bf16)
+        total = pick(a, i, 1).astype(f32)
         for step in range(1, inner):
-            total += along(
-                lax.dynamic_index_in_dim(a, (i + inner - step) % inner, 1, keepdims=False), 0, step
-            ).astype(f32)
-        a = total.astype(bf16)
-        total = lax.dynamic_index_in_dim(a, o, 0, keepdims=False).astype(f32)
+            total += along(pick(a, (i + inner - step) % inner, 1), 0, step).astype(f32)
+        return total.astype(bf16)
+
+    def reduce_line(a, o, *late):
+        terms = lax.optimization_barrier(tuple(pick(a, (o + outer - step) % outer, 0) for step in range(1, outer)))
+        total = pick(after(a, *late), o, 0).astype(f32)
         for step in range(1, outer):
-            total += along(
-                lax.dynamic_index_in_dim(a, (o + outer - step) % outer, 0, keepdims=False), step, 0
-            ).astype(f32)
-        a = total.astype(bf16)
-        total = a.astype(f32)
-        for step in range(1, X):
-            total += lax.ppermute(
-                a, "dp", [(d, (d + 2 * step) % dp_size) for d in range(dp_size)]
-            ).astype(f32)
+            total += along(terms[step - 1], step, 0).astype(f32)
         return total.astype(bf16)
+
+    def gather_x(a, x):
+        if X == 2:
+            other = across(a, 1)
+            return jnp.concatenate([jnp.where(x == 0, a, other), jnp.where(x == 0, other, a)], axis=0)
+        full = jnp.zeros((X,) + a.shape, a.dtype)
+        for step in range(X):
+            full = lax.dynamic_update_index_in_dim(full, across(a, step) if step else a, (x + step) % X, 0)
+        return full.reshape((X * a.shape[0],) + a.shape[1:])
 
     def local(
         inputs,
@@ -274,19 +446,20 @@
         part = width // F
         deep = hidden // F
         core = lax.axis_index("dp") % 2
+        x = lax.axis_index("dp") // 2
         f = lax.axis_index("fsdp")
         o, i = f // inner, f % inner
         is_first = core == 0
 
         def route(k, back):
             perm = []
-            for x in range(X):
+            for plane in range(X):
                 for c in range(2):
                     for b in range(F):
                         t = b % per_core
                         to_core = (b // per_core) % 2
                         to_chip = (c * seqs + (t ^ k)) * chips + b // (2 * per_core)
-                        pair = ((x * 2 + c) * F + b, (x * 2 + to_core) * F + to_chip)
+                        pair = ((plane * 2 + c) * F + b, (plane * 2 + to_core) * F + to_chip)
                         perm.append(pair[::-1] if back else pair)
             return perm
 
@@ -305,7 +478,7 @@
                 [lax.dynamic_index_in_dim(got, t ^ seq_here, 0) for t in range(per_core)], axis=0
             )
 
-        def to_blocks(a):
+        def to_blocks(a, *late):
             a = a.reshape(per_core, block, width)
             got = [
                 lax.ppermute(
@@ -313,6 +486,7 @@
                 )
                 for k in range(seqs)
             ]
+            got[0] = after(got[0], *late)
             got = jnp.stack(got)
             return jnp.concatenate(
                 [lax.dynamic_index_in_dim(got, s ^ slot, 0) for s in range(seqs)], axis=0
@@ -323,40 +497,47 @@
                 [jnp.where(is_first, mine, other), jnp.where(is_first, other, mine)], axis=axis
             )
 
-        small = jnp.concatenate(
-            [query_bias, value_bias, out_bias, norm1_gain, norm1_shift, down_bias, norm2_gain, norm2_shift, up_bias]
-        )
         heads_w = jnp.concatenate(
             [lax.dynamic_slice_in_dim(qkv_weight, n * width + core * half, half, 1) for n in range(3)], axis=1
         )
         lanes = heads_w.shape[1]
-        first_pack = jnp.concatenate(
-            [heads_w, jnp.pad(small[None], ((0, 7), (0, lanes - small.shape[0])))], axis=0
+
+        def x_rows(a):
+            rows = a.shape[0] // X
+            return lax.dynamic_slice_in_dim(a, x * rows, rows, 0)
+
+        slim = part // X
+        deep_rows = -(-deep // 128)
+        wide = -(-(8 + deep_rows) // slim)
+        singles = (query_bias, value_bias, out_bias, norm1_gain, norm1_shift, down_bias, norm2_gain, norm2_shift)
+        row = lax.broadcasted_iota(jnp.int32, (slim * wide, 128), 0)
+        small = jnp.pad(
+            jnp.pad(up_bias, (0, deep_rows * 128 - deep)).reshape(deep_rows, 128),
+            ((8, slim * wide - 8 - deep_rows), (0, 0)),
         )
-        first_all = gather(first_pack, o, i)
-        w_heads = first_all[:, :part].reshape(width, lanes)
-        small_all = first_all[:, part].astype(f32)
-        vectors = small_all[:, : 8 * part].reshape(F, 8, part).transpose(1, 0, 2).reshape(8, width)
-        b_query, b_value, b_out, gain1, shift1, b_down, gain2, shift2 = [vectors[n] for n in range(8)]
-        b_up_all = small_all[:, 8 * part : 8 * part + deep].reshape(F, 2, deep // 2)
+        for n, vector in enumerate(singles):
+            small = jnp.where(row == n, jnp.pad(vector, (0, 128 - part))[None, :], small)
+        first_line = gather_line(
+            jnp.concatenate([x_rows(heads_w), small.reshape(slim, wide * 128)], axis=1), o
+        )
+        first_sides = gather_sides(first_line)
 
         seg_row_own = jnp.pad(segments.astype(bf16)[:, None, :], ((0, 0), (0, 7), (0, width - block)))
         tokens = to_chips(jnp.concatenate([inputs, seg_row_own], axis=1))
         tokens_other = swap(tokens)
-        grad_low = to_chips(cotangent).reshape(own, width)
-
-        up_half = lax.dynamic_index_in_dim(
-            up_weight.reshape(part, F, 2, deep // 2), core, 2, keepdims=False
-        ).reshape(part, hidden // 2)
-        out_half = lax.dynamic_slice_in_dim(out_weight, core * half, half, 1)
-        down_half = lax.dynamic_slice_in_dim(down_weight, core * (deep // 2), deep // 2, 0)
-        second_all = gather(jnp.concatenate([up_half, out_half], axis=1), o, i).reshape(width, -1)
-        second_other = swap(second_all)
-        third_all = gather(down_half, o, i).reshape(hidden // 2, width)
-        third_other = swap(third_all)
-        ups = (second_all[:, : hidden // 2], second_other[:, : hidden // 2])
-        downs = (third_all, third_other)
-        w_out = in_order(second_all[:, hidden // 2 :], second_other[:, hidden // 2 :], 1)
+
+        first_all = gather_rest(first_line, first_sides, i, x)
+        w_heads = first_all.reshape(width, lanes + wide * 128)[:, :lanes]
+        small_all = first_all[:, :, 0, :, lanes:].reshape(F, slim * wide, 128)
+        vectors, b_up_all = unpack_small(small_all, part, deep)
+        b_query, b_value, b_out, gain1, shift1, b_down, gain2, shift2 = [vectors[n : n + 1] for n in range(8)]
+
+        up_half = pick(x_rows(up_weight).reshape(slim, F, 2, deep // 2), core, 2).reshape(slim, hidden // 2)
+        out_half = lax.dynamic_slice_in_dim(x_rows(out_weight), core * half, half, 1)
+        down_half = x_rows(lax.dynamic_slice_in_dim(down_weight, core * (deep // 2), deep // 2, 0))
+        second_pack = after(
+            jnp.concatenate([up_half, out_half], axis=1), tokens_other, first_line, *first_sides
+        )
 
         x_own = tokens[:, :block].reshape(own, width).astype(f32)
         x_all = in_order(
@@ -368,11 +549,15 @@
             tokens[:, block, :block].reshape(own), tokens_other[:, block, :block].reshape(own), 0
         ).astype(f32)
         joined = jnp.dot(hidden1, w_heads, preferred_element_type=f32)
-        bq = lax.dynamic_slice_in_dim(b_query, core * half, half)
-        bv = lax.dynamic_slice_in_dim(b_value, core * half, half)
+        bq = jnp.where(is_first, b_query[:, :half], b_query[:, half:])
+        bv = jnp.where(is_first, b_value[:, :half], b_value[:, half:])
         q = (joined[:, :half] + bq).astype(bf16) * bf16(HEAD_DIM ** (-0.5))
         k = joined[:, half : 2 * half].astype(bf16)
         v = (joined[:, 2 * half :] + bv).astype(bf16)
+        second_line = gather_line(second_pack, o, q)
+        second_sides = gather_sides(second_line)
+        third_pack = after(down_half, second_line)
+        q = after(q, second_line)
         if chips == 1:
             seg_col, seg_row = seg[:, None], seg[None, :]
             mixed, lse = attend(q, k, v, seg_col, seg_row)
@@ -387,49 +572,75 @@
             )
             mixed, lse = attend_far(q, k, v, allowed)
 
+        third_line = gather_line(third_pack, o, mixed)
+        third_sides = gather_sides(third_line)
+        second_sides = [after(t, mixed) for t in second_sides]
+        second_all = gather_rest(second_line, second_sides, i, x).reshape(width, -1)
+        second_other = swap(second_all)
+        third_all = gather_rest(third_line, third_sides, i, x).reshape(hidden // 2, width)
+        third_other = swap(third_all)
+        ups = (second_all[:, : hidden // 2], second_other[:, : hidden // 2])
+        downs = (third_all, third_other)
+        w_out = in_order(second_all[:, hidden // 2 :], second_other[:, hidden // 2 :], 1)
         mixed_other = swap(lax.dynamic_slice_in_dim(mixed, (1 - core) * own, own, 0))
         mixed_own = in_order(lax.dynamic_slice_in_dim(mixed, core * own, own, 0), mixed_other, 1)
+        mixed_own = after(mixed_own, third_line)
         midway = x_own + jnp.dot(mixed_own, w_out, preferred_element_type=f32) + b_out
         xhat2, inverse2 = standardize(midway)
         hidden2 = (xhat2 * gain2 + shift2).astype(bf16)
-        pre_acts, activs, pulls = [], [], []
+        activs, slopes = [], []
         result = midway + b_down
         for n in range(2):
-            b_up = lax.dynamic_index_in_dim(b_up_all, core ^ n, 1, keepdims=False).reshape(hidden // 2)
+            b_up = jnp.where(core == n, b_up_all[:1], b_up_all[1:])
             pre = jnp.dot(hidden2, ups[n], preferred_element_type=f32) + b_up
-            act, pull = jax.vjp(lambda t: jax.nn.gelu(t, approximate=True), pre)
-            act = act.astype(bf16)
-            activs.append(act)
-            pulls.append(pull)
-            result += jnp.dot(act, downs[n], preferred_element_type=f32)
-        output = to_blocks(result.astype(bf16))
+            square = pre * pre
+            bend = jnp.tanh(GELU_A * pre * (1.0 + GELU_B * square))
+            rise = 0.5 * (1.0 + bend)
+            activs.append((pre * rise).astype(bf16))
+            slope = rise + 0.5 * pre * (1.0 - bend * bend) * (GELU_A * (1.0 + 3.0 * GELU_B * square))
+            slopes.append(slope.astype(bf16))
+            result += jnp.dot(activs[n], downs[n], preferred_element_type=f32)
+        grad_low = to_chips(after(cotangent, *third_sides)).reshape(own, width)
+        result = result.astype(bf16)
 
         grad_out = grad_low.astype(f32)
-        d_down_b = jnp.sum(grad_out, axis=0)
+        d_down_b = jnp.sum(grad_out, axis=0, keepdims=True)
         d_pres = [None, None]
         d_downs = [None, None]
         d_ups = [None, None]
         for n in (1, 0):
             d_downs[n] = dot(activs[n], grad_low, 0, 0).astype(bf16)
-            d_pres[n] = pulls[n](dot(grad_low, downs[n], 1, 1))[0].astype(bf16)
+        d_down_other = swap(d_downs[1])
+        grad_next = after(grad_low, *d_downs)
+        for n in (1, 0):
+            d_pres[n] = (dot(grad_next, downs[n], 1, 1) * slopes[n].astype(f32)).astype(bf16)
             d_ups[n] = dot(hidden2, d_pres[n], 0, 0).astype(bf16)
-        d_down_sum = (d_downs[0].astype(f32) + swap(d_downs[1]).astype(f32)).astype(bf16)
-        d_down_red = reduce(d_down_sum.reshape(F, deep // 2, width), o, i)
-        d_hidden2 = dot(d_pres[0], ups[0], 1, 1) + dot(d_pres[1], ups[1], 1, 1)
-        d_up_bs = [jnp.sum(t.astype(f32), axis=0) for t in d_pres]
+        d_up_other = swap(d_ups[1])
+        d_down_sum = (after(d_downs[0], d_pres[1]).astype(f32) + d_down_other.astype(f32)).astype(bf16)
+        down_state = reduce_far(d_down_sum.reshape(outer, inner, X, deep // 2 // X, width), i, x)
+        d_pre = after(d_pres[0], *down_state[1])
+        d_hidden2 = dot(d_pre, ups[0], 1, 1) + dot(d_pres[1], ups[1], 1, 1)
+        d_up_bs = [jnp.sum(t.astype(f32), axis=0, keepdims=True) for t in d_pres]
         d_norm2, d_gain2, d_shift2 = norm_backward(d_hidden2, xhat2, inverse2, gain2)
         d_mid = grad_out + d_norm2
         d_branch = d_mid.astype(bf16)
         d_mixed = dot(d_branch, w_out, 1, 1).astype(bf16)
         d_mixed_other = swap(lax.dynamic_slice_in_dim(d_mixed, (1 - core) * half, half, 1))
         d_out = dot(mixed_own, d_branch, 0, 0).astype(bf16)
-        d_out_b = jnp.sum(d_branch.astype(f32), axis=0)
-        give = jnp.concatenate([d_ups[1], lax.dynamic_slice_in_dim(d_out, (1 - core) * half, half, 1)], axis=1)
-        keep = jnp.concatenate([d_ups[0], lax.dynamic_slice_in_dim(d_out, core * half, half, 1)], axis=1)
-        d_second = (keep.astype(f32) + swap(give).astype(f32)).astype(bf16)
-        d_second_red = reduce(d_second.reshape(F, part, -1), o, i)
+        d_out_b = jnp.sum(d_branch.astype(f32), axis=0, keepdims=True)
+        d_out_other = swap(lax.dynamic_slice_in_dim(d_out, (1 - core) * half, half, 1))
+        d_second = jnp.concatenate(
+            [
+                (d_ups[0].astype(f32) + d_up_other.astype(f32)).astype(bf16),
+                (lax.dynamic_slice_in_dim(d_out, core * half, half, 1).astype(f32) + d_out_other.astype(f32)).astype(bf16),
+            ],
+            axis=1,
+        )
+        second_state = reduce_far(d_second.reshape(outer, inner, X, slim, -1), i, x)
 
         d_heads = in_order(lax.dynamic_slice_in_dim(d_mixed, core * half, half, 1), d_mixed_other, 0)
+        down_plane = reduce_sides(down_state, i, x, (d_pres[0],), (d_mixed,))
+        d_heads = after(d_heads, d_second, down_plane)
         if chips == 1:
             dq, dk, dv = attend_back(q, k, v, d_heads, lse, seg_col, seg_row)
         else:
@@ -441,45 +652,49 @@
                 for t in (dk, dv)
             )
             dq = dq.astype(bf16)
+        output = to_blocks(result, dq)
+        dq = after(dq, *second_state[1])
+        d_down_red = reduce_line(down_plane, o, dq)
         d_joined = jnp.concatenate([dq, dk, dv], axis=1)
+        d_w_heads = dot(hidden1, d_joined, 0, 0)
         d_hidden1 = dot(d_joined, w_heads, 1, 1)
+        second_plane = reduce_sides(second_state, i, x, (dq,), (d_w_heads,))
+        d_second_red = reduce_line(second_plane, o)
         d_hidden1_other = swap(lax.dynamic_slice_in_dim(d_hidden1, (1 - core) * own, own, 0).astype(bf16))
         d_hidden1 = lax.dynamic_slice_in_dim(d_hidden1, core * own, own, 0) + d_hidden1_other.astype(f32)
         xhat1, inverse1 = standardize(x_own)
         d_norm1, d_gain1, d_shift1 = norm_backward(d_hidden1, xhat1, inverse1, gain1)
         d_inputs = to_blocks((d_mid + d_norm1).astype(bf16))
 
-        d_w_heads = dot(hidden1, d_joined, 0, 0)
-        d_bias = jnp.sum(d_joined.astype(f32), axis=0)
-
-        def placed(vector):
-            return lax.dynamic_update_slice_in_dim(jnp.zeros((width,), f32), vector, core * half, 0)
-
-        d_vectors = jnp.stack(
-            [placed(d_bias[:half]), placed(d_bias[2 * half :]), d_out_b, d_gain1, d_shift1, d_down_b, d_gain2, d_shift2]
-        )
-        d_vectors = d_vectors.reshape(8, F, part).transpose(1, 0, 2).reshape(F, 8 * part)
-        d_up_b = in_order(d_up_bs[0].reshape(F, 1, deep // 2), d_up_bs[1].reshape(F, 1, deep // 2), 1)
-        d_small = jnp.concatenate([d_vectors, d_up_b.reshape(F, deep)], axis=1)
-        d_small = jnp.pad(d_small[:, None], ((0, 0), (0, 7), (0, lanes - d_small.shape[1])))
-        d_first = jnp.concatenate([d_w_heads.reshape(F, part, lanes), d_small], axis=1).astype(bf16)
-        d_first_red = reduce(d_first, o, i)
-
-        first_o = swap(d_first_red)
-        second_o = swap(d_second_red)
-        down_o = swap(d_down_red)
+        d_bias = jnp.sum(d_joined.astype(f32), axis=0, keepdims=True)
+
+        d_small = pack_small(
+            core,
+            (d_out_b, d_gain1, d_shift1, d_down_b, d_gain2, d_shift2),
+            d_bias,
+            d_up_bs[0],
+            d_up_bs[1],
+            F,
+            slim * wide,
+        ).reshape(F, 1, slim, wide * 128)
+        d_small = jnp.pad(d_small, ((0, 0), (0, X - 1), (0, 0), (0, 0))).reshape(width, wide * 128)
+        d_first = jnp.concatenate([d_w_heads, d_small], axis=1).astype(bf16)
+        first_state = reduce_far(d_first.reshape(outer, inner, X, slim, lanes + wide * 128), i, x)
+        d_first_red = reduce_line(reduce_sides(first_state, i, x, (), ()), o)
+
+        d_first_red, d_second_red, d_down_red = [gather_x(t, x) for t in (d_first_red, d_second_red, d_down_red)]
+        first_o, second_o, down_o = [swap(t) for t in (d_first_red, d_second_red, d_down_red)]
         cols = half
         pieces = []
         for n in range(3):
             sl = slice(n * cols, (n + 1) * cols)
-            pieces.append(in_order(d_first_red[:part, sl], first_o[:part, sl], 1))
+            pieces.append(in_order(d_first_red[:, sl], first_o[:, sl], 1))
         d_qkv_w = jnp.concatenate(pieces, axis=1).astype(f32)
-        small_sum = d_first_red[part].astype(f32) + first_o[part].astype(f32)
-        vec = [small_sum[n * part : (n + 1) * part] for n in range(8)]
-        d_up_b = small_sum[8 * part : 8 * part + deep]
-        up_m = d_second_red[:, : hidden // 2].reshape(part, F, 1, deep // 2)
-        up_o = second_o[:, : hidden // 2].reshape(part, F, 1, deep // 2)
-        d_up_w = in_order(up_m, up_o, 2).reshape(part, hidden).astype(f32)
+        small_sum = d_first_red[:slim, lanes:].astype(f32) + first_o[:slim, lanes:].astype(f32)
+        small_sum = small_sum.reshape(slim * wide, 128)
+        vec = [small_sum[n, :part] for n in range(8)]
+        d_up_b = small_sum[8 : 8 + deep_rows].reshape(deep_rows * 128)[:deep]
+        d_up_w = weave(core, d_second_red[:, : hidden // 2], second_o[:, : hidden // 2], F)
         d_out_w = in_order(d_second_red[:, hidden // 2 :], second_o[:, hidden // 2 :], 1).astype(f32)
         d_down_w = in_order(d_down_red, down_o, 0).astype(f32)
         return (

time: 506 us -> 376 us (0.74)
  waiting for transfers between devices: 237 us -> 131 us
  matrix products: 62.3 us -> 35.8 us
  Pallas kernels: 27.8 us -> 41.1 us
  other arithmetic: 42.8 us -> 33.5 us
  local copies, waits for them, and re-layouts: 36.1 us -> 29.2 us
  starting transfers between devices: 91.1 us -> 97.5 us
    ppermute x24 -> x30, waiting for transfers between devices: 197 us -> 84.1 us  [along(): return lax.ppermute(a, 'fsdp', perm)]
    ppermute x3 -> x15, waiting for transfers between devices: 9.15 us -> 35.8 us  [across(): lax.ppermute(a, 'dp', [((d + 2 * step) % dp_size, d) for d in range(dp_si...]
    dot_general x12, matrix products: 46.4 us -> 24 us  [dot(): lax.dot_general(a, b, (((ca,), (cb,)), ((), ())), preferred_element_type=...]
    ppermute x8, waiting for transfers between devices: 16.2 us -> 0.77 us  [to_blocks(): lax.ppermute(lax.dynamic_index_in_dim(a, seq_here ^ k, 0, keepdims=False)...]
    pallas_call x0 -> x9, Pallas kernels: none -> 13.3 us  [the longest x6 7.93 us: place(): pl.pallas_call(kernel, out_shape=jax.ShapeDtypeStruct(shape, pieces[0].dt...]
    ppermute x8, starting transfers between devices: 18.3 us -> 29.1 us  [to_blocks(): lax.ppermute(lax.dynamic_index_in_dim(a, seq_here ^ k, 0, keepdims=False)...]
    another operation x7 -> x1, other arithmetic: 7.4 us -> 0.08 us  [place(): jnp.stack([jnp.asarray(v, jnp.int32) for index in indices for v in index])]
    dynamic_update_slice x12 -> x0, local copies, waits for them, and re-layouts: 6.23 us -> none  [the longest x10 6.2 us: gather(): line = lax.dynamic_update_index_in_dim(line, piece, (o + step) % outer, 0)]
  transfers between devices with their start and end apart: 54 -> 73, of which waited for: 25 -> 35; matrix products, arithmetic and copies ran while one was open for 18% -> 23% of each run, Pallas kernels for 6% -> 10%
where the time goes in v2:
time: 376 us; the launch traced here: 370 us
  waiting for transfers between devices  131 us (35%)
  starting transfers between devices  97.5 us (26%)
  Pallas kernels  41.1 us (11%)
  matrix products  35.8 us (10%)
  other arithmetic  33.5 us (9%)
  local copies, waits for them, and re-layouts  29.2 us (8%)
    ppermute x30, waiting for transfers between devices, along(): return lax.ppermute(a, 'fsdp', perm)  84.1 us
    ppermute x15, waiting for transfers between devices, across(): lax.ppermute(a, 'dp', [((d + 2 * step) % dp_size, d) for d in range(dp_si...  35.8 us
    ppermute x30, starting transfers between devices, along(): return lax.ppermute(a, 'fsdp', perm)  29.2 us
    ppermute x8, starting transfers between devices, to_blocks(): lax.ppermute(lax.dynamic_index_in_dim(a, seq_here ^ k, 0, keepdims=False)...  29.1 us
    dot_general x12, matrix products, dot(): lax.dot_general(a, b, (((ca,), (cb,)), ((), ())), preferred_element_type=...  24 us
    ppermute x8, starting transfers between devices, to_chips(): lax.ppermute(lax.dynamic_index_in_dim(a, slot ^ k, 0, keepdims=False), ('...  18.2 us
    pallas_call x1, Pallas kernels, attend_back(): pl.pallas_call(lambda *refs: attend_back_kernel(*refs, rows=min(256, leng...  18 us
    ppermute x12, starting transfers between devices, swap(): return lax.ppermute(a, 'dp', [(d, d ^ 1) for d in range(dp_size)])  13.3 us
  transfers between devices with their start and end apart: 73, of which 35 were waited for; matrix products, arithmetic and copies ran while one was open for 23% of the time, Pallas kernels for 10%

profile of v2, /device:TPU:9, one launch (start us, length us, event | category | flops | bytes accessed | tf_op | source)
XLA Modules:
  0.0 370.5 jit_solution(555637599873208392)
XLA Ops:
  13.2 4.3 %collective-permute-start.3 = (bf16[136,768]{1,0:T(8,128)(2,1)S(1)}, bf16[136,768]{1,0:T(8,128)(2,1)S(1)}, u32[]{:S(2)}, u32[]{:S(2)}) collective-permute-start(bf16[136,768]{1,0:T(8,128)(2,1)S(1)} %get-tuple-element.170), channel_id=1, source_target_pairs={{0,3},{1,2},{2,1},{3,0},{4,11},{5,10},{6,9},{7,8},{8,7},{9,6},{10,... | collective-permute-start | bytes 626696 | tf_op jit(solution)/shard_map/ppermute | solution.py:471
  18.5 3.5 collective-permute-start
  22.3 17.2 %collective-permute-done.7.refs_3_ = bf16[48,1280]{1,0:T(8,128)(2,1)S(1)} collective-permute-done((bf16[48,1280]{1,0:T(8,128)(2,1)S(1)}, bf16[48,1280]{1,0:T(8,128)(2,1)S(1)}, u32[]{:S(2)}, u32[]{:S(2)}) %collective-permute-start.7) | collective-permute-done | bytes 122912 | tf_op jit(solution)/shard_map/ppermute | solution.py:337
  46.6 3.1 collective-permute-done.9.refs_2_
  64.0 3.4 collective-permute-start.13
  77.1 3.6 collective-permute-done.14.refs_3_
  84.4 9.9 %attend.1 = (bf16[1024,384]{1,0:T(8,128)(2,1)S(1)}, f32[3,8,1024]{2,1,0:T(8,128)S(1)}) custom-call(bf16[1024,384]{1,0:T(8,128)(2,1)S(1)} %get-tuple-element.66.refs_0_, bf16[1024,384]{1,0:T(8,128)(2,1)S(1)} %get-tuple-element.136.refs_1_, bf16[1024,384]{1,0:T(8,128)(2,1)S(1)} %fusion.15.refs_2_, f32[1024,1]{1,0:T(8,128)S(1)} %convert_element_type.360.refs_3_.refs_5_, ...), custom_call_target="tpu_custom_call" | custom-call | flops 11274289152 | bytes 3145728 | tf_op jit(solution)/shard_map/attend/pallas_call | solution.py:96
  94.3 6.4 %collective-permute-done.19.refs_1_ = bf16[4,48,1920]{2,1,0:T(8,128)(2,1)S(1)} collective-permute-done((bf16[4,48,1920]{2,1,0:T(8,128)(2,1)S(1)}, bf16[4,48,1920]{2,1,0:T(8,128)(2,1)S(1)}, u32[]{:S(2)}, u32[]{:S(2)}) %collective-permute-start.19) | collective-permute-done | bytes 737312 | tf_op jit(solution)/shard_map/ppermute | solution.py:340
  102.5 7.3 %collective-permute-done.21.refs_3_ = bf16[2,48,1920]{2,1,0:T(8,128)(2,1)S(1)} collective-permute-done((bf16[2,48,1920]{2,1,0:T(8,128)(2,1)S(1)}, bf16[2,48,1920]{2,1,0:T(8,128)(2,1)S(1)}, u32[]{:S(2)}, u32[]{:S(2)}) %collective-permute-start.21) | collective-permute-done | bytes 368672 | tf_op jit(solution)/shard_map/ppermute | solution.py:340
  116.7 3.4 collective-permute-start.16
  124.3 5.4 %collective-permute-done.17.refs_2_ = bf16[96,768]{1,0:T(8,128)(2,1)S(1)} collective-permute-done((bf16[96,768]{1,0:T(8,128)(2,1)S(1)}, bf16[96,768]{1,0:T(8,128)(2,1)S(1)}, u32[]{:S(2)}, u32[]{:S(2)}) %collective-permute-start.17) | collective-permute-done | bytes 147488 | tf_op jit(solution)/shard_map/ppermute | solution.py:337
  129.7 3.2 collective-permute-done.18.refs_3_
  138.3 10.5 %collective-permute-done.24.refs_1_ = bf16[4,96,768]{2,1,0:T(8,128)(2,1)S(1)} collective-permute-done((bf16[4,96,768]{2,1,0:T(8,128)(2,1)S(1)}, bf16[4,96,768]{2,1,0:T(8,128)(2,1)S(1)}, u32[]{:S(2)}, u32[]{:S(2)}) %collective-permute-start.24) | collective-permute-done | bytes 589856 | tf_op jit(solution)/shard_map/ppermute | solution.py:340
  149.7 3.5 collective-permute-start.33
  155.7 3.4 collective-permute-start.30
  159.7 7.2 %collective-permute-done.32 = bf16[128,768]{1,0:T(8,128)(2,1)S(1)} collective-permute-done((bf16[128,768]{1,0:T(8,128)(2,1)S(1)}, bf16[128,768]{1,0:T(8,128)(2,1)S(1)}, u32[]{:S(2)}, u32[]{:S(2)}) %collective-permute-start.32) | collective-permute-done | bytes 196640 | tf_op jit(solution)/shard_map/ppermute | solution.py:471
  184.8 3.1 convert_reduce_fusion.2
  197.4 3.1 convert_reduce_fusion.3
  201.7 3.1 fusion.8
  207.6 6.2 %collective-permute-done.35 = bf16[2,96,768]{2,1,0:T(8,128)(2,1)S(1)} collective-permute-done((bf16[2,96,768]{2,1,0:T(8,128)(2,1)S(1)}, bf16[2,96,768]{2,1,0:T(8,128)(2,1)S(1)}, u32[]{:S(2)}, u32[]{:S(2)}) %collective-permute-start.35) | collective-permute-done | bytes 294944 | tf_op jit(solution)/shard_map/ppermute | solution.py:337
  226.2 10.4 %collective-permute-done.41 = bf16[4,96,768]{2,1,0:T(8,128)(2,1)S(1)} collective-permute-done((bf16[4,96,768]{2,1,0:T(8,128)(2,1)S(1)}, bf16[4,96,768]{2,1,0:T(8,128)(2,1)S(1)}, u32[]{:S(2)}, u32[]{:S(2)}) %collective-permute-start.41) | collective-permute-done | bytes 589856 | tf_op jit(solution)/shard_map/ppermute | solution.py:337
  236.6 5.3 %collective-permute-start.29 = (bf16[128,768]{1,0:T(8,128)(2,1)}, bf16[128,768]{1,0:T(8,128)(2,1)S(1)}, u32[]{:S(2)}, u32[]{:S(2)}) collective-permute-start(bf16[128,768]{1,0:T(8,128)(2,1)} %get-tuple-element.193), channel_id=1, source_target_pairs={{0,0},{1,1},{2,2},{3,3},{8,4},{9,5},{10,6},{11,7},{4,8},{5,9},{6,1... | collective-permute-start | bytes 589832 | tf_op jit(solution)/shard_map/ppermute | solution.py:484
  242.2 18.0 %attend_back.1 = (bf16[1024,384]{1,0:T(8,128)(2,1)S(1)}, bf16[1024,384]{1,0:T(8,128)(2,1)S(1)}, bf16[1024,384]{1,0:T(8,128)(2,1)S(1)}) custom-call(bf16[1024,384]{1,0:T(8,128)(2,1)S(1)} %copy-done.7, bf16[1024,384]{1,0:T(8,128)(2,1)S(1)} %copy-done.5, bf16[1024,384]{1,0:T(8,128)(2,1)S(1)} %copy-done.9, bf16[1024,384]{1,0:T(8,128)(2,1)S(1)} %pad_maximum_fusion.8.refs_3_, ...), custom_call_target="tpu_custom_call" | custom-call | flops 20132659200 | bytes 6291456 | tf_op jit(solution)/shard_map/attend_back/pallas_call | solution.py:123
  261.8 3.5 collective-permute-start.69
  287.2 9.1 %collective-permute-done.62 = bf16[4,48,1920]{2,1,0:T(8,128)(2,1)S(1)} collective-permute-done((bf16[4,48,1920]{2,1,0:T(8,128)(2,1)S(1)}, bf16[4,48,1920]{2,1,0:T(8,128)(2,1)S(1)}, u32[]{:S(2)}, u32[]{:S(2)}) %collective-permute-start.62) | collective-permute-done | bytes 737312 | tf_op jit(solution)/shard_map/ppermute | solution.py:337
  306.3 4.5 %collective-permute-start.51 = (bf16[128,768]{1,0:T(8,128)(2,1)}, bf16[128,768]{1,0:T(8,128)(2,1)S(1)}, u32[]{:S(2)}, u32[]{:S(2)}) collective-permute-start(bf16[128,768]{1,0:T(8,128)(2,1)} %get-tuple-element.178), channel_id=1, source_target_pairs={{3,0},{2,1},{1,2},{0,3},{11,4},{10,5},{9,6},{8,7},{7,8},{6,9},{5,1... | collective-permute-start | bytes 589832 | tf_op jit(solution)/shard_map/ppermute | solution.py:484
  314.6 4.0 %collective-permute-start.49 = (bf16[128,768]{1,0:T(8,128)(2,1)S(1)}, bf16[128,768]{1,0:T(8,128)(2,1)S(1)}, u32[]{:S(2)}, u32[]{:S(2)}) collective-permute-start(bf16[128,768]{1,0:T(8,128)(2,1)S(1)} %get-tuple-element.180), channel_id=1, source_target_pairs={{1,0},{0,1},{3,2},{2,3},{9,4},{8,5},{11,6},{10,7},{5,8},{4,9},{7,1... | collective-permute-start | bytes 589832 | tf_op jit(solution)/shard_map/ppermute | solution.py:484
  318.6 10.1 %collective-permute-start.48 = (bf16[128,768]{1,0:T(8,128)(2,1)S(1)}, bf16[128,768]{1,0:T(8,128)(2,1)S(1)}, u32[]{:S(2)}, u32[]{:S(2)}) collective-permute-start(bf16[128,768]{1,0:T(8,128)(2,1)S(1)} %get-tuple-element.177), channel_id=1, source_target_pairs={{0,0},{1,1},{2,2},{3,3},{8,4},{9,5},{10,6},{11,7},{4,8},{5,9},{6,1... | collective-permute-start | bytes 589832 | tf_op jit(solution)/shard_map/ppermute | solution.py:484
  338.8 7.2 %collective-permute-done.55 = bf16[4,48,1280]{2,1,0:T(8,128)(2,1)S(1)} collective-permute-done((bf16[4,48,1280]{2,1,0:T(8,128)(2,1)S(1)}, bf16[4,48,1280]{2,1,0:T(8,128)(2,1)S(1)}, u32[]{:S(2)}, u32[]{:S(2)}) %collective-permute-start.55) | collective-permute-done | bytes 491552 | tf_op jit(solution)/shard_map/ppermute | solution.py:337
  349.5 4.0 %collective-permute-start.67 = (bf16[96,1920]{1,0:T(8,128)(2,1)S(1)}, bf16[96,1920]{1,0:T(8,128)(2,1)S(1)}, u32[]{:S(2)}, u32[]{:S(2)}) collective-permute-start(bf16[96,1920]{1,0:T(8,128)(2,1)S(1)} %pad_maximum_fusion.21), channel_id=1, source_target_pairs={{0,8},{8,0},{16,24},{24,16},{1,9},{9,1},{17,25},{25,17},{2,10},{10... | collective-permute-start | bytes 1105928 | tf_op jit(solution)/shard_map/ppermute | solution.py:329
  353.5 3.6 collective-permute-done.57
  357.1 3.8 %collective-permute-done.56 = bf16[48,1280]{1,0:T(8,128)(2,1)S(1)} collective-permute-done((bf16[48,1280]{1,0:T(8,128)(2,1)S(1)}, bf16[48,1280]{1,0:T(8,128)(2,1)S(1)}, u32[]{:S(2)}, u32[]{:S(2)}) %collective-permute-start.56) | collective-permute-done | bytes 122912 | tf_op jit(solution)/shard_map/ppermute | solution.py:337
  (352 shorter events, 174.2 us)
Async XLA Ops:
  13.2 28.8 %collective-permute-start.3 = (bf16[136,768]{1,0:T(8,128)(2,1)S(1)}, bf16[136,768]{1,0:T(8,128)(2,1)S(1)}, u32[]{:S(2)}, u32[]{:S(2)}) collective-permute-start(bf16[136,768]{1,0:T(8,128)(2,1)S(1)} %get-tuple-element.170), channel_id=1, source_target_pairs={{0,3},{1,2},{2,1},{3,0},{4,11},{5,10},{6,9},{7,8},{8,7},{9,6},{10,... | collective-permute-start | bytes 626696 | tf_op jit(solution)/shard_map/ppermute | solution.py:471
  17.5 25.7 %collective-permute-start.2 = (bf16[136,768]{1,0:T(8,128)(2,1)}, bf16[136,768]{1,0:T(8,128)(2,1)S(1)}, u32[]{:S(2)}, u32[]{:S(2)}) collective-permute-start(bf16[136,768]{1,0:T(8,128)(2,1)} %get-tuple-element.171), channel_id=1, source_target_pairs={{0,2},{1,3},{2,0},{3,1},{4,10},{5,11},{6,8},{7,9},{8,6},{9,7},{10,... | collective-permute-start | bytes 626696 | tf_op jit(solution)/shard_map/ppermute | solution.py:471
  17.5 25.7 %collective-permute-start.1 = (bf16[136,768]{1,0:T(8,128)(2,1)}, bf16[136,768]{1,0:T(8,128)(2,1)}, u32[]{:S(2)}, u32[]{:S(2)}) collective-permute-start(bf16[136,768]{1,0:T(8,128)(2,1)} %get-tuple-element.172), channel_id=1, source_target_pairs={{0,1},{1,0},{2,3},{3,2},{4,9},{5,8},{6,11},{7,10},{8,5},{9,4},{10,... | collective-permute-start | bytes 626696 | tf_op jit(solution)/shard_map/ppermute | solution.py:471
  18.5 24.7 %collective-permute-start = (bf16[136,768]{1,0:T(8,128)(2,1)}, bf16[136,768]{1,0:T(8,128)(2,1)S(1)}, u32[]{:S(2)}, u32[]{:S(2)}) collective-permute-start(bf16[136,768]{1,0:T(8,128)(2,1)} %get-tuple-element.169), channel_id=1, source_target_pairs={{0,0},{1,1},{2,2},{3,3},{4,8},{5,9},{6,10},{7,11},{8,4},{9,5},{10,... | collective-permute-start | bytes 626696 | tf_op jit(solution)/shard_map/ppermute | solution.py:471
  22.1 17.4 %collective-permute-start.7 = (bf16[48,1280]{1,0:T(8,128)(2,1)S(1)}, bf16[48,1280]{1,0:T(8,128)(2,1)S(1)}, u32[]{:S(2)}, u32[]{:S(2)}) collective-permute-start(bf16[48,1280]{1,0:T(8,128)(2,1)S(1)} %pad_maximum_fusion.25.refs_0_), channel_id=1, source_target_pairs={{6,0},{7,1},{0,2},{1,3},{2,4},{3,5},{4,6},{5,7},{14,8},{15,9},{8,1... | collective-permute-start | bytes 368648 | tf_op jit(solution)/shard_map/ppermute | solution.py:337
  46.1 17.9 %collective-permute-start.4 = (bf16[4,136,768]{2,1,0:T(8,128)(2,1)}, bf16[4,136,768]{2,1,0:T(8,128)(2,1)}, u32[]{:S(2)}, u32[]{:S(2)}) collective-permute-start(bf16[4,136,768]{2,1,0:T(8,128)(2,1)} %pad_maximum_fusion.4), channel_id=1, source_target_pairs={{0,8},{8,0},{16,24},{24,16},{1,9},{9,1},{17,25},{25,17},{2,10},{10... | collective-permute-start | bytes 2506760 | tf_op jit(solution)/shard_map/ppermute | solution.py:329
  82.9 17.8 %collective-permute-start.19 = (bf16[4,48,1920]{2,1,0:T(8,128)(2,1)S(1)}, bf16[4,48,1920]{2,1,0:T(8,128)(2,1)S(1)}, u32[]{:S(2)}, u32[]{:S(2)}) collective-permute-start(bf16[4,48,1920]{2,1,0:T(8,128)(2,1)S(1)} %place.8.refs_0_), channel_id=1, source_target_pairs={{16,0},{24,8},{0,16},{8,24},{17,1},{25,9},{1,17},{9,25},{18,2},{26... | collective-permute-start | bytes 2211848 | tf_op jit(solution)/shard_map/ppermute | solution.py:340
  83.6 17.4 %collective-permute-start.20 = (bf16[4,48,1920]{2,1,0:T(8,128)(2,1)S(1)}, bf16[4,48,1920]{2,1,0:T(8,128)(2,1)S(1)}, u32[]{:S(2)}, u32[]{:S(2)}) collective-permute-start(bf16[4,48,1920]{2,1,0:T(8,128)(2,1)S(1)} %place.8.refs_0_), channel_id=1, source_target_pairs={{1,0},{0,1},{3,2},{2,3},{5,4},{4,5},{7,6},{6,7},{9,8},{8,9},{11,10... | collective-permute-start | bytes 2211848 | tf_op jit(solution)/shard_map/ppermute | solution.py:337
  111.6 61.9 %collective-permute-start.23 = (bf16[768,1920]{1,0:T(8,128)(2,1)S(1)}, bf16[768,1920]{1,0:T(8,128)(2,1)}, u32[]{:S(2)}, u32[]{:S(2)}) collective-permute-start(bf16[768,1920]{1,0:T(8,128)(2,1)S(1)} %bitcast.248), channel_id=1, source_target_pairs={{0,8},{8,0},{16,24},{24,16},{1,9},{9,1},{17,25},{25,17},{2,10},{10... | collective-permute-start | bytes 8847368 | tf_op jit(solution)/shard_map/ppermute | solution.py:329
  134.2 14.5 %collective-permute-start.24 = (bf16[4,96,768]{2,1,0:T(8,128)(2,1)S(1)}, bf16[4,96,768]{2,1,0:T(8,128)(2,1)S(1)}, u32[]{:S(2)}, u32[]{:S(2)}) collective-permute-start(bf16[4,96,768]{2,1,0:T(8,128)(2,1)S(1)} %place.9.refs_0_), channel_id=1, source_target_pairs={{16,0},{24,8},{0,16},{8,24},{17,1},{25,9},{1,17},{9,25},{18,2},{26... | collective-permute-start | bytes 1769480 | tf_op jit(solution)/shard_map/ppermute | solution.py:340
  135.5 14.1 %collective-permute-start.25 = (bf16[4,96,768]{2,1,0:T(8,128)(2,1)S(1)}, bf16[4,96,768]{2,1,0:T(8,128)(2,1)S(1)}, u32[]{:S(2)}, u32[]{:S(2)}) collective-permute-start(bf16[4,96,768]{2,1,0:T(8,128)(2,1)S(1)} %place.9.refs_0_), channel_id=1, source_target_pairs={{1,0},{0,1},{3,2},{2,3},{5,4},{4,5},{7,6},{6,7},{9,8},{8,9},{11,10... | collective-permute-start | bytes 1769480 | tf_op jit(solution)/shard_map/ppermute | solution.py:337
  137.1 18.6 %collective-permute-start.15 = (bf16[512,384]{1,0:T(8,128)(2,1)S(1)}, bf16[512,384]{1,0:T(8,128)(2,1)S(1)}, u32[]{:S(2)}, u32[]{:S(2)}) collective-permute-start(bf16[512,384]{1,0:T(8,128)(2,1)S(1)} %constant_dynamic-slice_fusion.15), channel_id=1, source_target_pairs={{0,8},{8,0},{16,24},{24,16},{1,9},{9,1},{17,25},{25,17},{2,10},{10... | collective-permute-start | bytes 1179656 | tf_op jit(solution)/shard_map/ppermute | solution.py:329
  181.1 23.7 %collective-permute-start.34 = (bf16[1536,768]{1,0:T(8,128)(2,1)S(1)}, bf16[1536,768]{1,0:T(8,128)(2,1)S(1)}, u32[]{:S(2)}, u32[]{:S(2)}) collective-permute-start(bf16[1536,768]{1,0:T(8,128)(2,1)S(1)} %convolution_convert_fusion.2), channel_id=1, source_target_pairs={{0,8},{8,0},{16,24},{24,16},{1,9},{9,1},{17,25},{25,17},{2,10},{10... | collective-permute-start | bytes 7077896 | tf_op jit(solution)/shard_map/ppermute | solution.py:329
  189.3 16.8 %collective-permute-start.38 = (bf16[768,1536]{1,0:T(8,128)(2,1)S(1)}, bf16[768,1536]{1,0:T(8,128)(2,1)S(1)}, u32[]{:S(2)}, u32[]{:S(2)}) collective-permute-start(bf16[768,1536]{1,0:T(8,128)(2,1)S(1)} %convolution_convert_fusion), channel_id=1, source_target_pairs={{0,8},{8,0},{16,24},{24,16},{1,9},{9,1},{17,25},{25,17},{2,10},{10... | collective-permute-start | bytes 7077896 | tf_op jit(solution)/shard_map/ppermute | solution.py:329
  194.4 67.4 %collective-permute-start.44 = (bf16[128,768]{1,0:T(8,128)(2,1)}, bf16[128,768]{1,0:T(8,128)(2,1)S(1)}, u32[]{:S(2)}, u32[]{:S(2)}) collective-permute-start(bf16[128,768]{1,0:T(8,128)(2,1)} %get-tuple-element.194), channel_id=1, source_target_pairs={{3,0},{2,1},{1,2},{0,3},{11,4},{10,5},{9,6},{8,7},{7,8},{6,9},{5,1... | collective-permute-start | bytes 589832 | tf_op jit(solution)/shard_map/ppermute | solution.py:484
  197.4 64.4 %collective-permute-start.43 = (bf16[128,768]{1,0:T(8,128)(2,1)}, bf16[128,768]{1,0:T(8,128)(2,1)S(1)}, u32[]{:S(2)}, u32[]{:S(2)}) collective-permute-start(bf16[128,768]{1,0:T(8,128)(2,1)} %get-tuple-element.195), channel_id=1, source_target_pairs={{2,0},{3,1},{0,2},{1,3},{10,4},{11,5},{8,6},{9,7},{6,8},{7,9},{4,1... | collective-permute-start | bytes 589832 | tf_op jit(solution)/shard_map/ppermute | solution.py:484
  220.0 16.6 %collective-permute-start.41 = (bf16[4,96,768]{2,1,0:T(8,128)(2,1)S(1)}, bf16[4,96,768]{2,1,0:T(8,128)(2,1)S(1)}, u32[]{:S(2)}, u32[]{:S(2)}) collective-permute-start(bf16[4,96,768]{2,1,0:T(8,128)(2,1)S(1)} %pad_maximum_fusion.18), channel_id=1, source_target_pairs={{1,0},{0,1},{3,2},{2,3},{5,4},{4,5},{7,6},{6,7},{9,8},{8,9},{11,10... | collective-permute-start | bytes 1769480 | tf_op jit(solution)/shard_map/ppermute | solution.py:337
  223.1 18.9 %collective-permute-start.40 = (bf16[4,96,768]{2,1,0:T(8,128)(2,1)S(1)}, bf16[4,96,768]{2,1,0:T(8,128)(2,1)S(1)}, u32[]{:S(2)}, u32[]{:S(2)}) collective-permute-start(bf16[4,96,768]{2,1,0:T(8,128)(2,1)S(1)} %pad_maximum_fusion.17), channel_id=1, source_target_pairs={{16,0},{24,8},{0,16},{8,24},{17,1},{25,9},{1,17},{9,25},{18,2},{26... | collective-permute-start | bytes 1769480 | tf_op jit(solution)/shard_map/ppermute | solution.py:340
  223.6 41.7 %collective-permute-start.42 = (bf16[128,768]{1,0:T(8,128)(2,1)}, bf16[128,768]{1,0:T(8,128)(2,1)S(1)}, u32[]{:S(2)}, u32[]{:S(2)}) collective-permute-start(bf16[128,768]{1,0:T(8,128)(2,1)} %get-tuple-element.196), channel_id=1, source_target_pairs={{1,0},{0,1},{3,2},{2,3},{9,4},{8,5},{11,6},{10,7},{5,8},{4,9},{7,1... | collective-permute-start | bytes 589832 | tf_op jit(solution)/shard_map/ppermute | solution.py:484
  236.6 23.6 %collective-permute-start.29 = (bf16[128,768]{1,0:T(8,128)(2,1)}, bf16[128,768]{1,0:T(8,128)(2,1)S(1)}, u32[]{:S(2)}, u32[]{:S(2)}) collective-permute-start(bf16[128,768]{1,0:T(8,128)(2,1)} %get-tuple-element.193), channel_id=1, source_target_pairs={{0,0},{1,1},{2,2},{3,3},{8,4},{9,5},{10,6},{11,7},{4,8},{5,9},{6,1... | collective-permute-start | bytes 589832 | tf_op jit(solution)/shard_map/ppermute | solution.py:484
  261.8 14.2 %collective-permute-start.70 = (bf16[96,768]{1,0:T(8,128)(2,1)S(1)}, bf16[96,768]{1,0:T(8,128)(2,1)S(1)}, u32[]{:S(2)}, u32[]{:S(2)}) collective-permute-start(bf16[96,768]{1,0:T(8,128)(2,1)S(1)} %get-tuple-element.110), channel_id=1, source_target_pairs={{6,0},{7,1},{0,2},{1,3},{2,4},{3,5},{4,6},{5,7},{14,8},{15,9},{8,1... | collective-permute-start | bytes 442376 | tf_op jit(solution)/shard_map/ppermute | solution.py:337
  261.8 14.2 %collective-permute-start.69 = (bf16[96,768]{1,0:T(8,128)(2,1)S(1)}, bf16[96,768]{1,0:T(8,128)(2,1)S(1)}, u32[]{:S(2)}, u32[]{:S(2)}) collective-permute-start(bf16[96,768]{1,0:T(8,128)(2,1)S(1)} %get-tuple-element.109), channel_id=1, source_target_pairs={{4,0},{5,1},{6,2},{7,3},{0,4},{1,5},{2,6},{3,7},{12,8},{13,9},{14,... | collective-permute-start | bytes 442376 | tf_op jit(solution)/shard_map/ppermute | solution.py:337
  275.8 25.7 %collective-permute-start.47 = (bf16[512,768]{1,0:T(8,128)(2,1)S(1)}, bf16[512,768]{1,0:T(8,128)(2,1)S(1)}, u32[]{:S(2)}, u32[]{:S(2)}) collective-permute-start(bf16[512,768]{1,0:T(8,128)(2,1)S(1)} %dynamic-slice_convert_fusion), channel_id=1, source_target_pairs={{0,8},{8,0},{16,24},{24,16},{1,9},{9,1},{17,25},{25,17},{2,10},{10... | collective-permute-start | bytes 2359304 | tf_op jit(solution)/shard_map/ppermute | solution.py:329
  278.7 17.7 %collective-permute-start.62 = (bf16[4,48,1920]{2,1,0:T(8,128)(2,1)S(1)}, bf16[4,48,1920]{2,1,0:T(8,128)(2,1)S(1)}, u32[]{:S(2)}, u32[]{:S(2)}) collective-permute-start(bf16[4,48,1920]{2,1,0:T(8,128)(2,1)S(1)} %pad_maximum_fusion.16), channel_id=1, source_target_pairs={{1,0},{0,1},{3,2},{2,3},{5,4},{4,5},{7,6},{6,7},{9,8},{8,9},{11,10... | collective-permute-start | bytes 2211848 | tf_op jit(solution)/shard_map/ppermute | solution.py:337
  279.9 18.9 %collective-permute-start.61 = (bf16[4,48,1920]{2,1,0:T(8,128)(2,1)S(1)}, bf16[4,48,1920]{2,1,0:T(8,128)(2,1)S(1)}, u32[]{:S(2)}, u32[]{:S(2)}) collective-permute-start(bf16[4,48,1920]{2,1,0:T(8,128)(2,1)S(1)} %pad_maximum_fusion.15), channel_id=1, source_target_pairs={{16,0},{24,8},{0,16},{8,24},{17,1},{25,9},{1,17},{9,25},{18,2},{26... | collective-permute-start | bytes 2211848 | tf_op jit(solution)/shard_map/ppermute | solution.py:340
  299.9 14.6 %collective-permute-start.65 = (bf16[48,1920]{1,0:T(8,128)(2,1)}, bf16[48,1920]{1,0:T(8,128)(2,1)}, u32[]{:S(2)}, u32[]{:S(2)}) collective-permute-start(bf16[48,1920]{1,0:T(8,128)(2,1)} %get-tuple-element.106), channel_id=1, source_target_pairs={{6,0},{7,1},{0,2},{1,3},{2,4},{3,5},{4,6},{5,7},{14,8},{15,9},{8,1... | collective-permute-start | bytes 552968 | tf_op jit(solution)/shard_map/ppermute | solution.py:337
  299.9 18.6 %collective-permute-start.64 = (bf16[48,1920]{1,0:T(8,128)(2,1)}, bf16[48,1920]{1,0:T(8,128)(2,1)}, u32[]{:S(2)}, u32[]{:S(2)}) collective-permute-start(bf16[48,1920]{1,0:T(8,128)(2,1)} %get-tuple-element.105), channel_id=1, source_target_pairs={{4,0},{5,1},{6,2},{7,3},{0,4},{1,5},{2,6},{3,7},{12,8},{13,9},{14,... | collective-permute-start | bytes 552968 | tf_op jit(solution)/shard_map/ppermute | solution.py:337
  301.5 27.2 %collective-permute-start.63 = (bf16[48,1920]{1,0:T(8,128)(2,1)}, bf16[48,1920]{1,0:T(8,128)(2,1)}, u32[]{:S(2)}, u32[]{:S(2)}) collective-permute-start(bf16[48,1920]{1,0:T(8,128)(2,1)} %get-tuple-element.104), channel_id=1, source_target_pairs={{2,0},{3,1},{4,2},{5,3},{6,4},{7,5},{0,6},{1,7},{10,8},{11,9},{12,... | collective-permute-start | bytes 552968 | tf_op jit(solution)/shard_map/ppermute | solution.py:337
  306.3 23.7 %collective-permute-start.51 = (bf16[128,768]{1,0:T(8,128)(2,1)}, bf16[128,768]{1,0:T(8,128)(2,1)S(1)}, u32[]{:S(2)}, u32[]{:S(2)}) collective-permute-start(bf16[128,768]{1,0:T(8,128)(2,1)} %get-tuple-element.178), channel_id=1, source_target_pairs={{3,0},{2,1},{1,2},{0,3},{11,4},{10,5},{9,6},{8,7},{7,8},{6,9},{5,1... | collective-permute-start | bytes 589832 | tf_op jit(solution)/shard_map/ppermute | solution.py:484
  310.7 21.1 %collective-permute-start.50 = (bf16[128,768]{1,0:T(8,128)(2,1)}, bf16[128,768]{1,0:T(8,128)(2,1)S(1)}, u32[]{:S(2)}, u32[]{:S(2)}) collective-permute-start(bf16[128,768]{1,0:T(8,128)(2,1)} %get-tuple-element.179), channel_id=1, source_target_pairs={{2,0},{3,1},{0,2},{1,3},{10,4},{11,5},{8,6},{9,7},{6,8},{7,9},{4,1... | collective-permute-start | bytes 589832 | tf_op jit(solution)/shard_map/ppermute | solution.py:484
  314.6 18.0 %collective-permute-start.49 = (bf16[128,768]{1,0:T(8,128)(2,1)S(1)}, bf16[128,768]{1,0:T(8,128)(2,1)S(1)}, u32[]{:S(2)}, u32[]{:S(2)}) collective-permute-start(bf16[128,768]{1,0:T(8,128)(2,1)S(1)} %get-tuple-element.180), channel_id=1, source_target_pairs={{1,0},{0,1},{3,2},{2,3},{9,4},{8,5},{11,6},{10,7},{5,8},{4,9},{7,1... | collective-permute-start | bytes 589832 | tf_op jit(solution)/shard_map/ppermute | solution.py:484
  318.6 14.8 %collective-permute-start.48 = (bf16[128,768]{1,0:T(8,128)(2,1)S(1)}, bf16[128,768]{1,0:T(8,128)(2,1)S(1)}, u32[]{:S(2)}, u32[]{:S(2)}) collective-permute-start(bf16[128,768]{1,0:T(8,128)(2,1)S(1)} %get-tuple-element.177), channel_id=1, source_target_pairs={{0,0},{1,1},{2,2},{3,3},{8,4},{9,5},{10,6},{11,7},{4,8},{5,9},{6,1... | collective-permute-start | bytes 589832 | tf_op jit(solution)/shard_map/ppermute | solution.py:484
  (68 other events, 681.3 us)
